TPU v7x, 768 devices: a whole 4x8x12 slice. The times are simulated.
768 devices in a mesh: gx: 12 (over z), gy: 4 (over x), gz: 16 (over y, core).
Axes of the slice: x: 4, y: 8, z: 12, core: 2. Of those that a mesh axis runs over, the one named last changes fastest.
Arguments:
- right_side: float32 [288, 128, 1024], P('gx', 'gz', 'gy'), may hold values from -40 to 40
- kappa: float32 [288, 128, 1024], P('gx', 'gz', 'gy'), may hold values from 0.5 to 4
Outputs:
- solution: float32 [288, 128, 1024], P('gx', 'gz', 'gy')
- residual: float32 [288, 128, 1024], P('gx', 'gz', 'gy')
- res_image: float32 [288, 128, 1024], P('gx', 'gz', 'gy')
- direction: float32 [288, 128, 1024], P('gx', 'gz', 'gy')
All inputs are finite; a program needn't handle non-finite values.
Results may differ from a plain program's by a relative error of at most 0.00025.
Values sent between devices are 32-bit elements; how exact they have to be, the bound alone decides.
A program may use at most 32 MiB of HBM per device.

v0:
```python
import jax
import jax.numpy as jnp
from jax import lax
from jax.sharding import PartitionSpec as P

ITERS = 4


def with_halo(block, sides, width):
    for axis, dim in sides:
        count = lax.axis_size(axis)
        forward = [(i, i + 1) for i in range(count - 1)]
        backward = [(target, source) for source, target in forward]
        low = lax.ppermute(
            lax.slice_in_dim(block, block.shape[dim] - width, None, axis=dim), axis, forward
        )
        high = lax.ppermute(lax.slice_in_dim(block, 0, width, axis=dim), axis, backward)
        block = jnp.concatenate([low, block, high], axis=dim)
    return block


def pad_coeff(kappa):
    return with_halo(kappa, (("gx", 0), ("gy", 2), ("gz", 1)), 1)


def pad_field(field):
    return with_halo(field, (("gx", 0), ("gy", 2), ("gz", 1)), 1)


def face_values(padded):
    centre = padded[1:-1, 1:-1, 1:-1]
    return (
        (centre + padded[2:, 1:-1, 1:-1]) * 0.5,
        (centre + padded[:-2, 1:-1, 1:-1]) * 0.5,
        (centre + padded[1:-1, 2:, 1:-1]) * 0.5,
        (centre + padded[1:-1, :-2, 1:-1]) * 0.5,
        (centre + padded[1:-1, 1:-1, 2:]) * 0.5,
        (centre + padded[1:-1, 1:-1, :-2]) * 0.5,
    )


def apply_padded(field, padded, stored_conds):
    total = stored_conds[0] * (field - padded[2:, 1:-1, 1:-1])
    total = total + stored_conds[1] * (field - padded[:-2, 1:-1, 1:-1])
    total = total + stored_conds[2] * (field - padded[1:-1, 2:, 1:-1])
    total = total + stored_conds[3] * (field - padded[1:-1, :-2, 1:-1])
    total = total + stored_conds[4] * (field - padded[1:-1, 1:-1, 2:])
    total = total + stored_conds[5] * (field - padded[1:-1, 1:-1, :-2])
    return total


def operate(field, stored_conds):
    return apply_padded(field, pad_field(field), stored_conds)


def global_sums(local_norm, local_inner):
    return lax.psum((local_norm, local_inner), ("gx", "gy", "gz"))


def shards(right_side, kappa):
    kappa_pad = pad_coeff(kappa)
    stored_conds = face_values(kappa_pad)
    res_image = operate(right_side, stored_conds)
    solution = jnp.zeros_like(right_side)
    residual = right_side
    direction = jnp.zeros_like(right_side)
    dir_image = jnp.zeros_like(right_side)
    dir_square = jnp.zeros_like(right_side)
    prior_norm = jnp.float32(1.0)
    prior_step = jnp.float32(1.0)
    for turn in range(ITERS):
        norm_now, inner = global_sums(jnp.sum(residual * residual), jnp.sum(res_image * residual))
        fresh = operate(res_image, stored_conds)
        if turn == 0:
            ratio = jnp.zeros_like(norm_now)
            step_len = norm_now / inner
        else:
            ratio = norm_now / prior_norm
            step_len = norm_now / (inner - ratio * norm_now / prior_step)
        dir_square = fresh + ratio * dir_square
        dir_image = res_image + ratio * dir_image
        direction = residual + ratio * direction
        solution = solution + step_len * direction
        residual = residual - step_len * dir_image
        res_image = res_image - step_len * dir_square
        prior_norm = norm_now
        prior_step = step_len
    return (solution, residual, res_image, direction)


def solution(mesh):
    placed = (P("gx", "gz", "gy"), P("gx", "gz", "gy"))
    return jax.shard_map(
        shards,
        mesh=mesh,
        in_specs=placed,
        out_specs=(
            P("gx", "gz", "gy"),
            P("gx", "gz", "gy"),
            P("gx", "gz", "gy"),
            P("gx", "gz", "gy"),
        ),
        check_vma=False,
    )
```

profile of v0, /device:TPU:1, one launch (start us, length us, event | category | flops | bytes accessed | tf_op | source)
XLA Modules:
  0.0 597.2 jit_solution(15727176798428652651)
XLA Ops:
  2.6 5.5 collective-permute-start.2
  10.1 4.6 collective-permute-start.3
  16.7 3.1 collective-permute-start.4
  22.5 4.6 collective-permute-start.7
  27.5 5.2 collective-permute-start.10
  32.7 6.4 %collective-permute-start.6 = (f32[26,1,258]{2,1,0:T(1,128)S(1)}, f32[26,1,258]{2,1,0:T(1,128)S(1)}, u32[]{:S(2)}, u32[]{:S(2)}) collective-permute-start(f32[26,1,258]{2,1,0:T(1,128)S(1)} %get-tuple-element.45), channel_id=1, source_target_pairs={{1,0},{2,1},{3,2},{4,3},{5,4},{6,5},{7,6},{8,7},{9,8},{10,9},{11,1... | collective-permute-start | bytes 80504 | tf_op jit(solution)/shard_map/ppermute | solution.py:17
  41.3 3.6 collective-permute-start.11
  47.3 3.3 collective-permute-start.13
  52.0 3.1 collective-permute-done.12
  56.4 4.3 collective-permute-start.14
  66.1 5.1 collective-permute-start.17
  71.2 117.5 %all-reduce.3 = (f32[]{:T(128)}, f32[]{:T(128)}) all-reduce(f32[]{:T(128)} %get-tuple-element.11, f32[]{:T(128)} %get-tuple-element.10), channel_id=1, replica_groups=mesh['gx'=12,'gy'=4,'gz'=16] {'gx','gy','gz'}, use_global_device_ids=true, to_apply=%region_1.0 | all-reduce | flops 2 | bytes 16 | tf_op jit(solution)/shard_map/psum | solution.py:57
  193.6 3.1 collective-permute-done.18
  198.1 4.0 collective-permute-start.20
  204.1 4.9 collective-permute-start.22
  210.9 109.2 %all-reduce.2 = (f32[]{:T(128)}, f32[]{:T(128)}) all-reduce(f32[]{:T(128)} %get-tuple-element.9, f32[]{:T(128)} %get-tuple-element.8), channel_id=1, replica_groups=mesh['gx'=12,'gy'=4,'gz'=16] {'gx','gy','gz'}, use_global_device_ids=true, to_apply=%region_5.0 | all-reduce | flops 2 | bytes 16 | tf_op jit(solution)/shard_map/psum | solution.py:57
  328.4 3.1 collective-permute-done.24
  332.9 4.0 collective-permute-start.26
  338.9 4.9 collective-permute-start.28
  343.7 3.7 collective-permute-start.29
  347.5 110.0 %all-reduce.1 = (f32[]{:T(128)}, f32[]{:T(128)}) all-reduce(f32[]{:T(128)} %get-tuple-element.7, f32[]{:T(128)} %get-tuple-element.6), channel_id=1, replica_groups=mesh['gx'=12,'gy'=4,'gz'=16] {'gx','gy','gz'}, use_global_device_ids=true, to_apply=%region_9.0 | all-reduce | flops 2 | bytes 16 | tf_op jit(solution)/shard_map/psum | solution.py:57
  469.6 4.0 collective-permute-start.32
  473.6 110.7 %all-reduce = (f32[]{:T(128)}, f32[]{:T(128)}) all-reduce(f32[]{:T(128)} %get-tuple-element.5, f32[]{:T(128)} %get-tuple-element.4), channel_id=1, replica_groups=mesh['gx'=12,'gy'=4,'gz'=16] {'gx','gy','gz'}, use_global_device_ids=true, to_apply=%region_13.0 | all-reduce | flops 2 | bytes 16 | tf_op jit(solution)/shard_map/psum | solution.py:57
  591.2 3.9 collective-permute-start.35
  (90 shorter events, 50.3 us)
Async XLA Ops:
  1.4 14.4 %collective-permute-start = (f32[1,8,256]{2,1,0:T(8,128)S(1)}, f32[1,8,256]{2,1,0:T(8,128)S(1)}, u32[]{:S(2)}, u32[]{:S(2)}) collective-permute-start(f32[1,8,256]{2,1,0:T(8,128)S(1)} %get-tuple-element.69), channel_id=1, source_target_pairs={{64,0},{128,64},{192,128},{256,192},{320,256},{384,320},{448,384},... | collective-permute-start | bytes 24584 | tf_op jit(solution)/shard_map/ppermute | solution.py:17
  2.6 12.1 %collective-permute-start.2 = (f32[1,8,256]{2,1,0:T(8,128)S(1)}, f32[1,8,256]{2,1,0:T(8,128)S(1)}, u32[]{:S(2)}, u32[]{:S(2)}) collective-permute-start(f32[1,8,256]{2,1,0:T(8,128)S(1)} %get-tuple-element.70), channel_id=1, source_target_pairs={{0,64},{64,128},{128,192},{192,256},{256,320},{320,384},{384,448},... | collective-permute-start | bytes 24584 | tf_op jit(solution)/shard_map/ppermute | solution.py:14
  8.8 12.3 %collective-permute-start.1 = (f32[1,8,256]{2,1,0:T(8,128)S(1)}, f32[1,8,256]{2,1,0:T(8,128)S(1)}, u32[]{:S(2)}, u32[]{:S(2)}) collective-permute-start(f32[1,8,256]{2,1,0:T(8,128)S(1)} %get-tuple-element.71), channel_id=1, source_target_pairs={{64,0},{128,64},{192,128},{256,192},{320,256},{384,320},{448,384},... | collective-permute-start | bytes 24584 | tf_op jit(solution)/shard_map/ppermute | solution.py:17
  10.1 5.7 collective-permute-start.3
  16.7 10.5 %collective-permute-start.4 = (f32[26,8,1]{2,1,0:T(8,128)S(1)}, f32[26,8,1]{2,1,0:T(8,128)S(1)}, u32[]{:S(2)}, u32[]{:S(2)}) collective-permute-start(f32[26,8,1]{2,1,0:T(8,128)S(1)} %get-tuple-element.57), channel_id=1, source_target_pairs={{0,16},{16,32},{32,48},{1,17},{17,33},{33,49},{2,18},{18,34},{34,5... | collective-permute-start | bytes 2504 | tf_op jit(solution)/shard_map/ppermute | solution.py:14
  19.8 7.4 %collective-permute-start.5 = (f32[26,8,1]{2,1,0:T(8,128)S(1)}, f32[26,8,1]{2,1,0:T(8,128)S(1)}, u32[]{:S(2)}, u32[]{:S(2)}) collective-permute-start(f32[26,8,1]{2,1,0:T(8,128)S(1)} %get-tuple-element.58), channel_id=1, source_target_pairs={{16,0},{32,16},{48,32},{17,1},{33,17},{49,33},{18,2},{34,18},{50,3... | collective-permute-start | bytes 2504 | tf_op jit(solution)/shard_map/ppermute | solution.py:17
  21.2 17.9 %collective-permute-start.8 = (f32[26,8,1]{2,1,0:T(8,128)S(1)}, f32[26,8,1]{2,1,0:T(8,128)S(1)}, u32[]{:S(2)}, u32[]{:S(2)}) collective-permute-start(f32[26,8,1]{2,1,0:T(8,128)S(1)} %get-tuple-element.59), channel_id=1, source_target_pairs={{16,0},{32,16},{48,32},{17,1},{33,17},{49,33},{18,2},{34,18},{50,3... | collective-permute-start | bytes 2504 | tf_op jit(solution)/shard_map/ppermute | solution.py:17
  22.5 16.6 %collective-permute-start.7 = (f32[26,8,1]{2,1,0:T(8,128)S(1)}, f32[26,8,1]{2,1,0:T(8,128)S(1)}, u32[]{:S(2)}, u32[]{:S(2)}) collective-permute-start(f32[26,8,1]{2,1,0:T(8,128)S(1)} %get-tuple-element.60), channel_id=1, source_target_pairs={{0,16},{16,32},{32,48},{1,17},{17,33},{33,49},{2,18},{18,34},{34,5... | collective-permute-start | bytes 2504 | tf_op jit(solution)/shard_map/ppermute | solution.py:14
  27.5 17.5 %collective-permute-start.10 = (f32[26,1,258]{2,1,0:T(1,128)S(1)}, f32[26,1,258]{2,1,0:T(1,128)S(1)}, u32[]{:S(2)}, u32[]{:S(2)}) collective-permute-start(f32[26,1,258]{2,1,0:T(1,128)S(1)} %get-tuple-element.44), channel_id=1, source_target_pairs={{0,1},{1,2},{2,3},{3,4},{4,5},{5,6},{6,7},{7,8},{8,9},{9,10},{10,1... | collective-permute-start | bytes 80504 | tf_op jit(solution)/shard_map/ppermute | solution.py:14
  32.7 12.3 %collective-permute-start.6 = (f32[26,1,258]{2,1,0:T(1,128)S(1)}, f32[26,1,258]{2,1,0:T(1,128)S(1)}, u32[]{:S(2)}, u32[]{:S(2)}) collective-permute-start(f32[26,1,258]{2,1,0:T(1,128)S(1)} %get-tuple-element.45), channel_id=1, source_target_pairs={{1,0},{2,1},{3,2},{4,3},{5,4},{6,5},{7,6},{8,7},{9,8},{10,9},{11,1... | collective-permute-start | bytes 80504 | tf_op jit(solution)/shard_map/ppermute | solution.py:17
  39.4 5.6 collective-permute-start.9
  55.1 7.0 %collective-permute-start.15 = (f32[26,8,1]{2,1,0:T(8,128)S(1)}, f32[26,8,1]{2,1,0:T(8,128)S(1)}, u32[]{:S(2)}, u32[]{:S(2)}) collective-permute-start(f32[26,8,1]{2,1,0:T(8,128)S(1)} %get-tuple-element.55), channel_id=1, source_target_pairs={{16,0},{32,16},{48,32},{17,1},{33,17},{49,33},{18,2},{34,18},{50,3... | collective-permute-start | bytes 2504 | tf_op jit(solution)/shard_map/ppermute | solution.py:17
  56.4 6.7 %collective-permute-start.14 = (f32[26,8,1]{2,1,0:T(8,128)S(1)}, f32[26,8,1]{2,1,0:T(8,128)S(1)}, u32[]{:S(2)}, u32[]{:S(2)}) collective-permute-start(f32[26,8,1]{2,1,0:T(8,128)S(1)} %get-tuple-element.56), channel_id=1, source_target_pairs={{0,16},{16,32},{32,48},{1,17},{17,33},{33,49},{2,18},{18,34},{34,5... | collective-permute-start | bytes 2504 | tf_op jit(solution)/shard_map/ppermute | solution.py:14
  63.4 126.6 %collective-permute-start.16 = (f32[26,1,258]{2,1,0:T(1,128)S(1)}, f32[26,1,258]{2,1,0:T(1,128)S(1)}, u32[]{:S(2)}, u32[]{:S(2)}) collective-permute-start(f32[26,1,258]{2,1,0:T(1,128)S(1)} %get-tuple-element.42), channel_id=1, source_target_pairs={{1,0},{2,1},{3,2},{4,3},{5,4},{6,5},{7,6},{8,7},{9,8},{10,9},{11,1... | collective-permute-start | bytes 80504 | tf_op jit(solution)/shard_map/ppermute | solution.py:17
  66.1 123.9 %collective-permute-start.17 = (f32[26,1,258]{2,1,0:T(1,128)S(1)}, f32[26,1,258]{2,1,0:T(1,128)S(1)}, u32[]{:S(2)}, u32[]{:S(2)}) collective-permute-start(f32[26,1,258]{2,1,0:T(1,128)S(1)} %get-tuple-element.43), channel_id=1, source_target_pairs={{0,1},{1,2},{2,3},{3,4},{4,5},{5,6},{6,7},{7,8},{8,9},{9,10},{10,1... | collective-permute-start | bytes 80504 | tf_op jit(solution)/shard_map/ppermute | solution.py:14
  198.1 5.7 collective-permute-start.20
  204.1 120.6 %collective-permute-start.22 = (f32[26,1,258]{2,1,0:T(1,128)S(1)}, f32[26,1,258]{2,1,0:T(1,128)S(1)}, u32[]{:S(2)}, u32[]{:S(2)}) collective-permute-start(f32[26,1,258]{2,1,0:T(1,128)S(1)} %get-tuple-element.40), channel_id=1, source_target_pairs={{1,0},{2,1},{3,2},{4,3},{5,4},{6,5},{7,6},{8,7},{9,8},{10,9},{11,1... | collective-permute-start | bytes 80504 | tf_op jit(solution)/shard_map/ppermute | solution.py:17
  209.0 115.8 %collective-permute-start.23 = (f32[26,1,258]{2,1,0:T(1,128)S(1)}, f32[26,1,258]{2,1,0:T(1,128)S(1)}, u32[]{:S(2)}, u32[]{:S(2)}) collective-permute-start(f32[26,1,258]{2,1,0:T(1,128)S(1)} %get-tuple-element.41), channel_id=1, source_target_pairs={{0,1},{1,2},{2,3},{3,4},{4,5},{5,6},{6,7},{7,8},{8,9},{9,10},{10,1... | collective-permute-start | bytes 80504 | tf_op jit(solution)/shard_map/ppermute | solution.py:14
  332.9 5.7 collective-permute-start.26
  338.9 122.6 %collective-permute-start.28 = (f32[26,1,258]{2,1,0:T(1,128)S(1)}, f32[26,1,258]{2,1,0:T(1,128)S(1)}, u32[]{:S(2)}, u32[]{:S(2)}) collective-permute-start(f32[26,1,258]{2,1,0:T(1,128)S(1)} %get-tuple-element.38), channel_id=1, source_target_pairs={{1,0},{2,1},{3,2},{4,3},{5,4},{6,5},{7,6},{8,7},{9,8},{10,9},{11,1... | collective-permute-start | bytes 80504 | tf_op jit(solution)/shard_map/ppermute | solution.py:17
  343.7 117.8 %collective-permute-start.29 = (f32[26,1,258]{2,1,0:T(1,128)S(1)}, f32[26,1,258]{2,1,0:T(1,128)S(1)}, u32[]{:S(2)}, u32[]{:S(2)}) collective-permute-start(f32[26,1,258]{2,1,0:T(1,128)S(1)} %get-tuple-element.39), channel_id=1, source_target_pairs={{0,1},{1,2},{2,3},{3,4},{4,5},{5,6},{6,7},{7,8},{8,9},{9,10},{10,1... | collective-permute-start | bytes 80504 | tf_op jit(solution)/shard_map/ppermute | solution.py:14
  468.3 120.0 %collective-permute-start.33 = (f32[26,8,1]{2,1,0:T(8,128)S(1)}, f32[26,8,1]{2,1,0:T(8,128)S(1)}, u32[]{:S(2)}, u32[]{:S(2)}) collective-permute-start(f32[26,8,1]{2,1,0:T(8,128)S(1)} %get-tuple-element.49), channel_id=1, source_target_pairs={{16,0},{32,16},{48,32},{17,1},{33,17},{49,33},{18,2},{34,18},{50,3... | collective-permute-start | bytes 2504 | tf_op jit(solution)/shard_map/ppermute | solution.py:17
  469.6 118.7 %collective-permute-start.32 = (f32[26,8,1]{2,1,0:T(8,128)S(1)}, f32[26,8,1]{2,1,0:T(8,128)S(1)}, u32[]{:S(2)}, u32[]{:S(2)}) collective-permute-start(f32[26,8,1]{2,1,0:T(8,128)S(1)} %get-tuple-element.50), channel_id=1, source_target_pairs={{0,16},{16,32},{32,48},{1,17},{17,33},{33,49},{2,18},{18,34},{34,5... | collective-permute-start | bytes 2504 | tf_op jit(solution)/shard_map/ppermute | solution.py:14
  588.6 7.4 %collective-permute-start.34 = (f32[26,1,258]{2,1,0:T(1,128)S(1)}, f32[26,1,258]{2,1,0:T(1,128)S(1)}, u32[]{:S(2)}, u32[]{:S(2)}) collective-permute-start(f32[26,1,258]{2,1,0:T(1,128)S(1)} %get-tuple-element.36), channel_id=1, source_target_pairs={{1,0},{2,1},{3,2},{4,3},{5,4},{6,5},{7,6},{8,7},{9,8},{10,9},{11,1... | collective-permute-start | bytes 80504 | tf_op jit(solution)/shard_map/ppermute | solution.py:17
  (14 other events, 64.9 us)
where the time goes:
time: 605 us; the launch traced here: 597 us
  blocking collectives  447 us (74%)
  starting transfers between devices  103 us (17%)
  waiting for transfers between devices  19.4 us (3%)
  between operations  15.1 us (2%)
  other arithmetic  8.01 us (1%)
    psum x4, blocking collectives, global_sums(): return lax.psum((local_norm, local_inner), ('gx', 'gy', 'gz'))  447 us
    ppermute x18, starting transfers between devices, with_halo(): lax.ppermute(lax.slice_in_dim(block, block.shape[dim] - width, None, axis...  64.6 us
    ppermute x18, starting transfers between devices, with_halo(): lax.ppermute(lax.slice_in_dim(block, 0, width, axis=dim), axis, backward)  38.8 us
    ppermute x18, waiting for transfers between devices, with_halo(): lax.ppermute(lax.slice_in_dim(block, 0, width, axis=dim), axis, backward)  14.1 us
  transfers between devices with their start and end apart: 36, of which 12 were waited for; matrix products, arithmetic and copies ran while one was open for 1% of the time, Pallas kernels for 0%

commit v1 on v0

v1 whole, which is shorter than its diff:
```python
import functools

import jax
import jax.numpy as jnp
from jax import lax
from jax.experimental import pallas as pl
from jax.experimental.pallas import tpu as pltpu
from jax.sharding import PartitionSpec as P

MESH = pl.DeviceIdType.MESH
F32 = jnp.float32
NX, NZ, NY = 24, 8, 256
LANES = 128
GRAM = ((0, 1), (0, 2), (0, 3), (1, 1), (1, 2), (1, 3), (2, 2), (2, 3), (3, 3), (3, 4))


def shifted(axis, step):
    count = lax.axis_size(axis)
    return {axis: lax.rem(lax.axis_index(axis) + (step + count), count)}


def ring(step, count):
    return min(step % count, (-step) % count)


def group_line():
    lines = lax.axis_size("gx")
    gx, gz = lax.axis_index("gx"), lax.axis_index("gz")
    core = lax.rem(gz, 2)
    offsets = [(d, c) for d in range(lines) for c in range(2) if (d, c) != (0, 0)]
    offsets.sort(key=lambda o: -(2 * ring(o[0], lines) + o[1]))
    peers = [
        {"gx": lax.rem(gx + d, lines), "gz": gz - core + lax.rem(core + c, 2)} for d, c in offsets
    ]
    return gx * 2 + core, 2 * lines, peers


def group_plane():
    wide, deep = lax.axis_size("gy"), lax.axis_size("gz") // 2
    gy, gz = lax.axis_index("gy"), lax.axis_index("gz")
    offsets = [(d, e) for d in range(deep) for e in range(wide) if (d, e) != (0, 0)]
    offsets.sort(key=lambda o: -(ring(o[0], deep) + ring(o[1], wide)))
    peers = [
        {"gy": lax.rem(gy + e, wide), "gz": lax.rem(gz + 2 * d, 2 * deep)} for d, e in offsets
    ]
    return (gz // 2) * wide + gy, wide * deep, peers


def full(value):
    return jnp.broadcast_to(value, (NZ, LANES))


def total(value):
    return jnp.sum(jnp.sum(value, axis=0, keepdims=True), axis=1, keepdims=True)


def to_row(values):
    lane = lax.broadcasted_iota(jnp.int32, (1, LANES), 1)
    row = jnp.zeros((1, LANES), F32)
    for at, value in enumerate(values):
        row = jnp.where(lane == at, jnp.broadcast_to(total(value), (1, LANES)), row)
    return row


def solve(gram, c, s2):
    zero = jnp.zeros_like(c)
    one = jnp.ones_like(c)

    def g(i, j):
        return gram[(min(i, j), max(i, j))]

    gram = dict(gram)
    gram[(0, 4)] = g(1, 3) - s2 * g(0, 2)
    gram[(1, 4)] = g(2, 3) + s2 * (g(0, 3) - g(1, 2))
    gram[(2, 4)] = g(3, 3) + s2 * (g(1, 3) - g(2, 2))

    def image(a, top):
        out = []
        for i in range(top + 2):
            term = None
            if i <= top:
                term = c * a[i]
            if i >= 1:
                term = a[i - 1] if term is None else term + a[i - 1]
            if i + 1 <= top:
                term = term + s2 * a[i + 1]
            out.append(term)
        return out

    energy = {}
    for i in range(4):
        for j in range(i, 4):
            term = g(i, j + 1) + c * g(i, j)
            if j >= 1:
                term = term + s2 * g(i, j - 1)
            energy[(i, j)] = term

    def form(matrix, a, top):
        out = None
        for i in range(top + 1):
            part = matrix[(i, i)] * a[i]
            for j in range(i + 1, top + 1):
                part = part + (matrix[(i, j)] * 2.0) * a[j]
            out = a[i] * part if out is None else out + a[i] * part
        return out

    rho, way, answer = [one], [], []
    prior_norm = prior_step = None
    for turn in range(4):
        norm_now = form(gram, rho, turn)
        inner = form(energy, rho, turn)
        if turn == 0:
            step = norm_now / inner
            way = list(rho)
        else:
            ratio = norm_now / prior_norm
            step = norm_now / (inner - ratio * norm_now / prior_step)
            way = [rho[i] + ratio * way[i] if i < turn else rho[i] for i in range(turn + 1)]
        answer = [answer[i] + step * way[i] if i < turn else step * way[i] for i in range(turn + 1)]
        moved = image(way, turn)
        rho = [rho[i] - step * moved[i] if i <= turn else zero - step * moved[i] for i in range(turn + 2)]
        prior_norm, prior_step = norm_now, step
    third = image(rho[:4], 3)
    return answer, rho, third + [rho[4]], way


def main_kernel(b_hbm, k_hbm, w_hbm, coef_ref,
                V, K, W, CX, CZL, CZH, CYL, CYH, XS0, XR0, ZS, ZR, YS, YR, RS, RA, RB,
                copy_sem, out_sem, halo_send, halo_recv, red_send, red_recv):
    gx, gy, gz = lax.axis_index("gx"), lax.axis_index("gy"), lax.axis_index("gz")
    core = lax.rem(gz, 2)
    rank_a, count_a, peers_a = group_line()
    rank_b, count_b, peers_b = group_plane()
    across = {"gz": lax.rem(gz + 2 * core - 1 + lax.axis_size("gz"), lax.axis_size("gz"))}

    barrier = pltpu.get_barrier_semaphore()
    greeted = peers_b + peers_a + [across]
    for peer in greeted:
        pl.semaphore_signal(barrier, inc=1, device_id=peer, device_id_type=MESH)

    loads = []
    for half in (0, 1):
        at = slice(half * LANES, (half + 1) * LANES)
        loads.append(pltpu.make_async_copy(b_hbm.at[:, :, at], V.at[0, 1:NX + 1, half], copy_sem.at[0, half]))
        loads.append(pltpu.make_async_copy(k_hbm.at[:, :, at], K.at[1:NX + 1, half], copy_sem.at[1, half]))
    for load in loads:
        load.start()

    lane = lax.broadcasted_iota(jnp.int32, (NZ, LANES), 1)
    row = lax.broadcasted_iota(jnp.int32, (NZ, LANES), 0)
    inside = {
        ("gx", 0): gx > 0, ("gx", 1): gx < lax.axis_size("gx") - 1,
        ("gy", 0): gy > 0, ("gy", 1): gy < lax.axis_size("gy") - 1,
        ("gz", 0): gz > 0, ("gz", 1): gz < lax.axis_size("gz") - 1,
    }
    target = {
        (axis, slot): shifted(axis, 1 if slot == 0 else -1) for axis in ("gx", "gy", "gz") for slot in (0, 1)
    }
    order = [("gz", 0), ("gz", 1), ("gx", 0), ("gx", 1), ("gy", 0), ("gy", 1)]

    def copies(phase):
        out = {}
        for at, (axis, slot) in enumerate(order):
            if axis == "gx":
                if phase == 0:
                    src, dst = XS0.at[slot], XR0.at[slot]
                else:
                    src = V.at[phase, NX if slot == 0 else 1]
                    dst = V.at[phase, 0 if slot == 0 else NX + 1]
            elif axis == "gz":
                src, dst = ZS[min(phase, 1)], ZR[min(phase, 1)]
                src, dst = (src.at[slot], dst.at[slot]) if phase == 0 else (src.at[phase, slot], dst.at[phase, slot])
            else:
                src, dst = YS[min(phase, 1)], YR[min(phase, 1)]
                src, dst = (src.at[slot], dst.at[slot]) if phase == 0 else (src.at[phase, slot], dst.at[phase, slot])
            out[(axis, slot)] = pltpu.make_async_remote_copy(
                src_ref=src, dst_ref=dst, send_sem=halo_send.at[phase, at], recv_sem=halo_recv.at[phase, at],
                device_id=target[(axis, slot)], device_id_type=MESH,
            )
        return out

    def edge_rows(flat, dst, at):
        for half in (0, 1):
            dst[half] = flat[pl.ds(2 * NZ + half * NZ + at, NX, stride=2 * NZ), :]

    def start_halo(phase):
        flat = V.at[phase].reshape((NX + 2) * 2 * NZ, LANES)
        edge_rows(flat, ZS[1].at[phase, 0], NZ - 1)
        edge_rows(flat, ZS[1].at[phase, 1], 0)
        sent = copies(phase)
        for name in order:
            sent[name].start()
        return sent

    def keep(flag, value):
        return jnp.where(flag, value, jnp.zeros_like(value))

    def end_halo(phase, sent):
        for name in order:
            sent[name].wait_recv()
        V[phase, 0] = keep(inside[("gx", 0)], V[phase, 0])
        V[phase, NX + 1] = keep(inside[("gx", 1)], V[phase, NX + 1])
        for slot in (0, 1):
            ZR[1][phase, slot] = keep(inside[("gz", slot)], ZR[1][phase, slot])
        return [keep(inside[("gy", slot)], YR[1][phase, slot]) for slot in (0, 1)]

    def tiles(ref, *at):
        return ref[(*at, 0)], ref[(*at, 1)]

    def put(ref, at, pair):
        ref[(*at, 0)], ref[(*at, 1)] = pair

    def lanes_down(pair, packed, x):
        first, second = pltpu.roll(pair[0], 1, 1), pltpu.roll(pair[1], 1, 1)
        edge = pltpu.roll(packed, lax.rem(LANES - x, LANES), 1)
        return jnp.where(lane == 0, edge, first), jnp.where(lane == 0, first, second)

    def lanes_up(pair, packed, x):
        first, second = pltpu.roll(pair[0], LANES - 1, 1), pltpu.roll(pair[1], LANES - 1, 1)
        edge = pltpu.roll(packed, LANES - 1 - x, 1)
        return jnp.where(lane == LANES - 1, second, first), jnp.where(lane == LANES - 1, edge, second)

    def rows_down(pair, halo):
        return tuple(jnp.where(row == 0, full(h), pltpu.roll(p, 1, 0)) for p, h in zip(pair, halo))

    def rows_up(pair, halo):
        return tuple(jnp.where(row == NZ - 1, full(h), pltpu.roll(p, NZ - 1, 0)) for p, h in zip(pair, halo))

    def halo_row(ref, at, x):
        return tuple(ref[(*at, half, pl.ds(x, 1), slice(None))] for half in (0, 1))

    def pack_edges(pair, packed, x):
        up = jnp.where(lane == x, pltpu.roll(pair[1], lax.rem(x + 1, LANES), 1), packed[0])
        down = jnp.where(lane == x, pltpu.roll(pair[0], x, 1), packed[1])
        return up, down

    blank = jnp.zeros((NZ, LANES), F32)

    def loop(body, carry):
        return lax.fori_loop(0, NX, body, carry, unroll=True)

    for load in loads:
        load.wait()

    def pack_both(x, packed):
        field = pack_edges(tiles(V, 0, x + 1), packed[:2], x)
        coeff = pack_edges(tiles(K, x + 1), packed[2:], x)
        return field + coeff

    packed = loop(pack_both, (blank,) * 4)
    YS[0][0, 0], YS[0][1, 0], YS[0][0, 1], YS[0][1, 1] = packed
    flat_v = V.at[0].reshape((NX + 2) * 2 * NZ, LANES)
    flat_k = K.reshape((NX + 2) * 2 * NZ, LANES)
    for slot, at, x in ((0, NZ - 1, NX), (1, 0, 1)):
        edge_rows(flat_v, ZS[0].at[slot, 0], at)
        edge_rows(flat_k, ZS[0].at[slot, 1], at)
        XS0[slot, 0] = V[0, x]
        XS0[slot, 1] = K[x]

    pl.semaphore_wait(barrier, len(greeted))
    everything = []
    sent = copies(0)
    for name in order:
        sent[name].start()
    everything += [sent[name] for name in order]
    for name in order:
        sent[name].wait_recv()
    for slot, x in ((0, 0), (1, NX + 1)):
        V[0, x] = keep(inside[("gx", slot)], XR0[slot, 0])
        K[x] = keep(inside[("gx", slot)], XR0[slot, 1])
        for what in (0, 1):
            ZR[0][slot, what] = keep(inside[("gz", slot)], ZR[0][slot, what])
    edges_k = [keep(inside[("gy", slot)], YR[0][slot, 1]) for slot in (0, 1)]
    edges_v = [keep(inside[("gy", slot)], YR[0][slot, 0]) for slot in (0, 1)]

    put(CX, (0,), tuple((a + b) * 0.5 for a, b in zip(tiles(K, 0), tiles(K, 1))))

    def conds(x, carry):
        here = tiles(K, x + 1)
        for ref, other in (
            (CX.at[x + 1], tiles(K, x + 2)),
            (CZL.at[x], rows_down(here, halo_row(ZR[0], (0, 1), x))),
            (CZH.at[x], rows_up(here, halo_row(ZR[0], (1, 1), x))),
            (CYL.at[x], lanes_down(here, edges_k[0], x)),
            (CYH.at[x], lanes_up(here, edges_k[1], x)),
        ):
            put(ref, (), tuple((a + b) * 0.5 for a, b in zip(here, other)))
        return carry

    loop(conds, 0)

    def stencil(src, zref, zat, edges, write, carry):
        def body(x, state):
            before, inner = state
            here = tiles(src, x + 1)
            after = tuple(c * (n - h) for c, n, h in zip(tiles(CX, x + 1), tiles(src, x + 2), here))
            out = tuple(a - b for a, b in zip(before, after))
            for cond, other in (
                (CZL, rows_down(here, halo_row(zref, zat[0], x))),
                (CZH, rows_up(here, halo_row(zref, zat[1], x))),
                (CYL, lanes_down(here, edges[0], x)),
                (CYH, lanes_up(here, edges[1], x)),
            ):
                out = tuple(o + c * (h - n) for o, c, h, n in zip(out, tiles(cond, x), here, other))
            return after, write(x, out, here, inner)

        first = tuple(c * (n - h) for c, n, h in zip(tiles(CX, 0), tiles(src, 1), tiles(src, 0)))
        return loop(body, (first, carry))[1]

    def advance(phase, edges, zref, zat, with_sums):
        def write(x, out, here, carry):
            put(V, (phase + 1, x + 1), out)
            packed, sums = carry
            packed = pack_edges(out, packed, x)
            if with_sums:
                sums = (
                    sums[0] + here[0] * here[0] + here[1] * here[1],
                    sums[1] + here[0] * out[0] + here[1] * out[1],
                    sums[2] + out[0] * out[0] + out[1] * out[1],
                )
            return packed, sums

        start = ((blank, blank), (blank, blank, blank) if with_sums else ())
        packed, sums = stencil(V.at[phase], zref, zat, edges, write, start)
        YS[1][phase + 1, 0], YS[1][phase + 1, 1] = packed
        return sums

    def send_sum(at, which, values):
        rank, count, peers, ref = (
            (rank_a, count_a, peers_a, RA) if which == 0 else (rank_b, count_b, peers_b, RB)
        )
        RS[at, which] = values
        for peer in peers:
            pltpu.make_async_remote_copy(
                src_ref=RS.at[at, which], dst_ref=ref.at[at, rank], send_sem=red_send.at[at, which],
                recv_sem=red_recv.at[at, which], device_id=peer, device_id_type=MESH,
            ).start()
        ref[at, rank] = values
        whole = ref.at[at, 0:count - 1]
        return pltpu.make_async_remote_copy(
            src_ref=whole, dst_ref=whole, send_sem=red_send.at[at, which], recv_sem=red_recv.at[at, which],
            device_id=peers[0], device_id_type=MESH,
        )

    def end_sum(at, which, waits):
        waits.wait_recv()
        return jnp.sum((RA if which == 0 else RB)[at], axis=0)

    sums = advance(0, edges_v, ZR[0], ((0, 0), (1, 0)), True)
    sent = start_halo(1)
    first_a = send_sum(0, 0, to_row(sums))
    everything += [sent[name] for name in order] + [first_a]

    advance(1, end_halo(1, sent), ZR[1], ((1, 0), (1, 1)), False)
    sent = start_halo(2)
    first_b = send_sum(0, 1, end_sum(0, 0, first_a))
    everything += [sent[name] for name in order] + [first_b]

    advance(2, end_halo(2, sent), ZR[1], ((2, 0), (2, 1)), False)
    sent = start_halo(3)
    everything += [sent[name] for name in order]
    advance(3, end_halo(3, sent), ZR[1], ((3, 0), (3, 1)), False)

    moments = end_sum(0, 1, first_b)
    m0, m1, m2 = (full(moments[:, at:at + 1]) for at in range(3))
    c = m1 / m0
    s2 = jnp.maximum(m2 / m0 - c * c, 0.0)

    def basis(x, carry):
        packed, sums = carry
        powers = [tiles(V, at, x + 1) for at in range(5)]
        fields = []
        for half in (0, 1):
            v = [power[half] for power in powers]
            one = [v[at + 1] - c * v[at] for at in range(4)]
            two = [one[at + 1] - c * one[at] - s2 * v[at] for at in range(3)]
            three = [two[at + 1] - c * two[at] - s2 * one[at] for at in range(2)]
            four = three[1] - c * three[0] - s2 * two[0]
            fields.append((v[0], one[0], two[0], three[0], four))
        for at in range(1, 4):
            put(W, (at - 1, x), (fields[0][at], fields[1][at]))
        last = (fields[0][4], fields[1][4])
        put(V, (4, x + 1), last)
        sums = tuple(
            s + fields[0][i] * fields[0][j] + fields[1][i] * fields[1][j] for s, (i, j) in zip(sums, GRAM)
        )
        return pack_edges(last, packed, x), sums

    packed, sums = loop(basis, ((blank, blank), (blank,) * len(GRAM)))
    second_a = send_sum(1, 0, to_row(sums))
    YS[1][4, 0], YS[1][4, 1] = packed
    sent = start_halo(4)
    everything += [sent[name] for name in order] + [second_a]
    stores = [pltpu.make_async_copy(V.at[0, 1:NX + 1], w_hbm.at[0], out_sem.at[0])]
    stores += [pltpu.make_async_copy(W.at[at - 1], w_hbm.at[at], out_sem.at[at]) for at in range(1, 4)]
    stores += [pltpu.make_async_copy(V.at[4, 1:NX + 1], w_hbm.at[4], out_sem.at[4])]
    for store in stores:
        store.start()

    def last_image(x, out, here, carry):
        put(W, (3, x), out)
        return carry

    stencil(V.at[4], ZR[1], ((4, 0), (4, 1)), end_halo(4, sent), last_image, 0)
    stores += [pltpu.make_async_copy(W.at[3], w_hbm.at[5], out_sem.at[5])]
    stores[-1].start()

    second_b = send_sum(1, 1, end_sum(1, 0, second_a))
    everything += [second_b]
    entries = end_sum(1, 1, second_b)
    gram = {pair: full(entries[:, at:at + 1]) for at, pair in enumerate(GRAM)}
    gram[(0, 0)] = m0
    at = 0
    for part in solve(gram, c, s2):
        for value in part:
            coef_ref[at] = value
            at += 1

    for store in stores:
        store.wait()
    for copy in everything:
        copy.wait_send()


def combine_kernel(w_ref, coef_ref, solution_ref, residual_ref, image_ref, direction_ref):
    for x in range(solution_ref.shape[0]):
        for half in (0, 1):
            at = slice(half * LANES, (half + 1) * LANES)
            w = [w_ref[i, x, half] for i in range(6)]
            start = 0
            for ref, count in ((solution_ref, 4), (residual_ref, 5), (image_ref, 6), (direction_ref, 4)):
                out = coef_ref[start] * w[0]
                for i in range(1, count):
                    out = out + coef_ref[start + i] * w[i]
                ref[x, :, at] = out
                start += count


def shards(right_side, kappa):
    line, plane = 2 * lax.axis_size("gx"), lax.axis_size("gy") * lax.axis_size("gz") // 2
    hbm = pl.BlockSpec(memory_space=pl.ANY)
    vmem = pl.BlockSpec(memory_space=pltpu.VMEM)
    block, inner = (NX, NZ, NY), (NX, 2, NZ, LANES)
    basis, coefs = pl.pallas_call(
        main_kernel,
        out_shape=(jax.ShapeDtypeStruct((6,) + inner, F32), jax.ShapeDtypeStruct((19, NZ, LANES), F32)),
        in_specs=[hbm, hbm],
        out_specs=(hbm, vmem),
        scratch_shapes=[
            pltpu.VMEM((5, NX + 2, 2, NZ, LANES), F32),
            pltpu.VMEM((NX + 2, 2, NZ, LANES), F32),
            pltpu.VMEM((4,) + inner, F32),
            pltpu.VMEM((NX + 1, 2, NZ, LANES), F32),
            pltpu.VMEM(inner, F32),
            pltpu.VMEM(inner, F32),
            pltpu.VMEM(inner, F32),
            pltpu.VMEM(inner, F32),
            pltpu.VMEM((2, 2, 2, NZ, LANES), F32),
            pltpu.VMEM((2, 2, 2, NZ, LANES), F32),
            [pltpu.VMEM((2, 2, 2, NX, LANES), F32), pltpu.VMEM((5, 2, 2, NX, LANES), F32)],
            [pltpu.VMEM((2, 2, 2, NX, LANES), F32), pltpu.VMEM((5, 2, 2, NX, LANES), F32)],
            [pltpu.VMEM((2, 2, NZ, LANES), F32), pltpu.VMEM((5, 2, NZ, LANES), F32)],
            [pltpu.VMEM((2, 2, NZ, LANES), F32), pltpu.VMEM((5, 2, NZ, LANES), F32)],
            pltpu.VMEM((2, 2, 1, LANES), F32),
            pltpu.VMEM((2, line, 1, LANES), F32),
            pltpu.VMEM((2, plane, 1, LANES), F32),
            pltpu.SemaphoreType.DMA((2, 2)),
            pltpu.SemaphoreType.DMA((6,)),
            pltpu.SemaphoreType.DMA((5, 6)),
            pltpu.SemaphoreType.DMA((5, 6)),
            pltpu.SemaphoreType.DMA((2, 2)),
            pltpu.SemaphoreType.DMA((2, 2)),
        ],
        compiler_params=pltpu.CompilerParams(collective_id=0, has_side_effects=True),
        name="basis_and_sums",
    )(right_side, kappa)
    part = 8
    out_block = pl.BlockSpec((part, NZ, NY), lambda i: (i, 0, 0))
    return pl.pallas_call(
        combine_kernel,
        grid=(NX // part,),
        out_shape=(jax.ShapeDtypeStruct(block, F32),) * 4,
        in_specs=[
            pl.BlockSpec((6, part, 2, NZ, LANES), lambda i: (0, i, 0, 0, 0)),
            pl.BlockSpec((19, NZ, LANES), lambda i: (0, 0, 0)),
        ],
        out_specs=(out_block,) * 4,
        name="combine",
    )(basis, coefs)


def solution(mesh):
    placed = P("gx", "gz", "gy")
    return jax.shard_map(
        shards,
        mesh=mesh,
        in_specs=(placed, placed),
        out_specs=(placed,) * 4,
        check_vma=False,
    )
```

time: 605 us -> 53 us (0.09); the launches traced: 597 us -> 52.8 us
  blocking collectives: 447 us -> 0 us
  starting transfers between devices: 103 us -> 0 us
  Pallas kernels: 0 us -> 52.1 us
  waiting for transfers between devices: 19.4 us -> 0 us
  between operations: 15.1 us -> 0.64 us
  other arithmetic: 8.01 us -> 0 us
    psum x4 -> x0, blocking collectives: 447 us -> none  [global_sums(): return lax.psum((local_norm, local_inner), ('gx', 'gy', 'gz'))]
    ppermute x36 -> x0, starting transfers between devices: 103 us -> none  [the longest x18 64.6 us: with_halo(): lax.ppermute(lax.slice_in_dim(block, block.shape[dim] - width, None, axis...]
    pallas_call x0 -> x2, Pallas kernels: none -> 52.1 us  [the longest x1 49.1 us: shards(): pl.pallas_call(main_kernel, out_shape=(jax.ShapeDtypeStruct((6,) + inner,...]
    ppermute x36 -> x0, waiting for transfers between devices: 19.4 us -> none  [the longest x18 14.1 us: with_halo(): lax.ppermute(lax.slice_in_dim(block, 0, width, axis=dim), axis, backward)]
  transfers between devices with their start and end apart: 36 -> 0, of which waited for: 12 -> 0; matrix products, arithmetic and copies ran while one was open for 1% -> 0% of each run, Pallas kernels for 0% -> 0%
where the time goes in v1:
time: 53 us; the launch traced here: 52.8 us
  Pallas kernels  52.1 us (98%)
  between operations  0.64 us (1%)
    pallas_call x1, Pallas kernels, shards(): pl.pallas_call(main_kernel, out_shape=(jax.ShapeDtypeStruct((6,) + inner,...  49.1 us
    pallas_call x1, Pallas kernels, shards(): pl.pallas_call(combine_kernel, grid=(NX // part,), out_shape=(jax.ShapeDt...  3.05 us

profile of v1, /device:TPU:1, one launch (start us, length us, event | category | flops | bytes accessed | tf_op | source)
XLA Modules:
  0.0 52.8 jit_solution(15721010893249559063)
XLA Ops:
  0.6 49.1 %basis_and_sums.1 = (f32[6,24,2,8,128]{4,3,2,1,0:T(8,128)}, f32[19,8,128]{2,1,0:T(8,128)}) custom-call(f32[24,8,256]{2,1,0:T(8,128)} %b_hbm.1, f32[24,8,256]{2,1,0:T(8,128)} %k_hbm.1), custom_call_target="tpu_custom_call" | custom-call | tf_op jit(solution)/shard_map/basis_and_sums/pallas_call | solution.py:444
  49.7 3.1 %combine.1 = (f32[24,8,256]{2,1,0:T(8,128)}, f32[24,8,256]{2,1,0:T(8,128)}, f32[24,8,256]{2,1,0:T(8,128)}, f32[24,8,256]{2,1,0:T(8,128)}) custom-call(f32[6,24,2,8,128]{4,3,2,1,0:T(8,128)} %get-tuple-element.6.w_ref, f32[19,8,128]{2,1,0:T(8,128)} %get-tuple-element.7.coef_ref), custom_call_target="tpu_custom_call" | custom-call | tf_op jit(solution)/shard_map/combine/pallas_call | solution.py:479

commit v2 on v1

--- a/solution.py
+++ b/solution.py
@@ -11,6 +11,7 @@
 F32 = jnp.float32
 NX, NZ, NY = 24, 8, 256
 LANES = 128
+PART = 12
 GRAM = ((0, 1), (0, 2), (0, 3), (1, 1), (1, 2), (1, 3), (2, 2), (2, 3), (3, 3), (3, 4))
 
 
@@ -124,19 +125,14 @@
     return answer, rho, third + [rho[4]], way
 
 
-def main_kernel(b_hbm, k_hbm, w_hbm, coef_ref,
-                V, K, W, CX, CZL, CZH, CYL, CYH, XS0, XR0, ZS, ZR, YS, YR, RS, RA, RB,
-                copy_sem, out_sem, halo_send, halo_recv, red_send, red_recv):
+def main_kernel(b_hbm, k_hbm, w_ref, coef_ref,
+                V, K, CX, CZL, CZH, CYL, CYH, XS0, XR0, ZS, ZR, YS, YR, RS, RA, RB,
+                copy_sem, halo_send, halo_recv, red_send, red_recv):
     gx, gy, gz = lax.axis_index("gx"), lax.axis_index("gy"), lax.axis_index("gz")
     core = lax.rem(gz, 2)
     rank_a, count_a, peers_a = group_line()
     rank_b, count_b, peers_b = group_plane()
     across = {"gz": lax.rem(gz + 2 * core - 1 + lax.axis_size("gz"), lax.axis_size("gz"))}
-
-    barrier = pltpu.get_barrier_semaphore()
-    greeted = peers_b + peers_a + [across]
-    for peer in greeted:
-        pl.semaphore_signal(barrier, inc=1, device_id=peer, device_id_type=MESH)
 
     loads = []
     for half in (0, 1):
@@ -145,6 +141,11 @@
         loads.append(pltpu.make_async_copy(k_hbm.at[:, :, at], K.at[1:NX + 1, half], copy_sem.at[1, half]))
     for load in loads:
         load.start()
+
+    barrier = pltpu.get_barrier_semaphore()
+    greeted = peers_b + peers_a + [across]
+    for peer in greeted:
+        pl.semaphore_signal(barrier, inc=1, device_id=peer, device_id_type=MESH)
 
     lane = lax.broadcasted_iota(jnp.int32, (NZ, LANES), 1)
     row = lax.broadcasted_iota(jnp.int32, (NZ, LANES), 0)
@@ -378,9 +379,11 @@
             four = three[1] - c * three[0] - s2 * two[0]
             fields.append((v[0], one[0], two[0], three[0], four))
         for at in range(1, 4):
-            put(W, (at - 1, x), (fields[0][at], fields[1][at]))
+            put(w_ref, (at, x), (fields[0][at], fields[1][at]))
         last = (fields[0][4], fields[1][4])
         put(V, (4, x + 1), last)
+        put(w_ref, (0, x), (fields[0][0], fields[1][0]))
+        put(w_ref, (4, x), last)
         sums = tuple(
             s + fields[0][i] * fields[0][j] + fields[1][i] * fields[1][j] for s, (i, j) in zip(sums, GRAM)
         )
@@ -391,20 +394,12 @@
     YS[1][4, 0], YS[1][4, 1] = packed
     sent = start_halo(4)
     everything += [sent[name] for name in order] + [second_a]
-    stores = [pltpu.make_async_copy(V.at[0, 1:NX + 1], w_hbm.at[0], out_sem.at[0])]
-    stores += [pltpu.make_async_copy(W.at[at - 1], w_hbm.at[at], out_sem.at[at]) for at in range(1, 4)]
-    stores += [pltpu.make_async_copy(V.at[4, 1:NX + 1], w_hbm.at[4], out_sem.at[4])]
-    for store in stores:
-        store.start()
 
     def last_image(x, out, here, carry):
-        put(W, (3, x), out)
+        put(w_ref, (5, x), out)
         return carry
 
     stencil(V.at[4], ZR[1], ((4, 0), (4, 1)), end_halo(4, sent), last_image, 0)
-    stores += [pltpu.make_async_copy(W.at[3], w_hbm.at[5], out_sem.at[5])]
-    stores[-1].start()
-
     second_b = send_sum(1, 1, end_sum(1, 0, second_a))
     everything += [second_b]
     entries = end_sum(1, 1, second_b)
@@ -416,40 +411,46 @@
             coef_ref[at] = value
             at += 1
 
-    for store in stores:
-        store.wait()
     for copy in everything:
         copy.wait_send()
 
 
-def combine_kernel(w_ref, coef_ref, solution_ref, residual_ref, image_ref, direction_ref):
-    for x in range(solution_ref.shape[0]):
-        for half in (0, 1):
-            at = slice(half * LANES, (half + 1) * LANES)
-            w = [w_ref[i, x, half] for i in range(6)]
-            start = 0
-            for ref, count in ((solution_ref, 4), (residual_ref, 5), (image_ref, 6), (direction_ref, 4)):
-                out = coef_ref[start] * w[0]
-                for i in range(1, count):
-                    out = out + coef_ref[start + i] * w[i]
-                ref[x, :, at] = out
-                start += count
+def combine_kernel(w_ref, coef_ref, solution_ref, residual_ref, image_ref, direction_ref, held, sems):
+    refs = (solution_ref, residual_ref, image_ref, direction_ref)
+    copies = []
+    for part in range(NX // PART):
+        for x in range(part * PART, (part + 1) * PART):
+            for half in (0, 1):
+                at = slice(half * LANES, (half + 1) * LANES)
+                w = [w_ref[i, x, half] for i in range(6)]
+                start = 0
+                for which, count in enumerate((4, 5, 6, 4)):
+                    out = coef_ref[start] * w[0]
+                    for i in range(1, count):
+                        out = out + coef_ref[start + i] * w[i]
+                    held[which, x, :, at] = out
+                    start += count
+        rows = pl.ds(part * PART, PART)
+        for which, ref in enumerate(refs):
+            copies.append(pltpu.make_async_copy(held.at[which, rows], ref.at[rows], sems.at[which, part]))
+            copies[-1].start()
+    for copy in copies:
+        copy.wait()
 
 
 def shards(right_side, kappa):
     line, plane = 2 * lax.axis_size("gx"), lax.axis_size("gy") * lax.axis_size("gz") // 2
-    hbm = pl.BlockSpec(memory_space=pl.ANY)
+    hbm = pl.BlockSpec(memory_space=pltpu.MemorySpace.HBM)
     vmem = pl.BlockSpec(memory_space=pltpu.VMEM)
     block, inner = (NX, NZ, NY), (NX, 2, NZ, LANES)
     basis, coefs = pl.pallas_call(
         main_kernel,
-        out_shape=(jax.ShapeDtypeStruct((6,) + inner, F32), jax.ShapeDtypeStruct((19, NZ, LANES), F32)),
+        out_shape=(pltpu.VMEM((6,) + inner, F32), pltpu.VMEM((19, NZ, LANES), F32)),
         in_specs=[hbm, hbm],
-        out_specs=(hbm, vmem),
+        out_specs=(vmem, vmem),
         scratch_shapes=[
             pltpu.VMEM((5, NX + 2, 2, NZ, LANES), F32),
             pltpu.VMEM((NX + 2, 2, NZ, LANES), F32),
-            pltpu.VMEM((4,) + inner, F32),
             pltpu.VMEM((NX + 1, 2, NZ, LANES), F32),
             pltpu.VMEM(inner, F32),
             pltpu.VMEM(inner, F32),
@@ -465,26 +466,21 @@
             pltpu.VMEM((2, line, 1, LANES), F32),
             pltpu.VMEM((2, plane, 1, LANES), F32),
             pltpu.SemaphoreType.DMA((2, 2)),
-            pltpu.SemaphoreType.DMA((6,)),
             pltpu.SemaphoreType.DMA((5, 6)),
             pltpu.SemaphoreType.DMA((5, 6)),
             pltpu.SemaphoreType.DMA((2, 2)),
             pltpu.SemaphoreType.DMA((2, 2)),
         ],
-        compiler_params=pltpu.CompilerParams(collective_id=0, has_side_effects=True),
+        compiler_params=pltpu.CompilerParams(collective_id=0, has_side_effects=True, vmem_limit_bytes=60 * 2**20),
         name="basis_and_sums",
     )(right_side, kappa)
-    part = 8
-    out_block = pl.BlockSpec((part, NZ, NY), lambda i: (i, 0, 0))
     return pl.pallas_call(
         combine_kernel,
-        grid=(NX // part,),
         out_shape=(jax.ShapeDtypeStruct(block, F32),) * 4,
-        in_specs=[
-            pl.BlockSpec((6, part, 2, NZ, LANES), lambda i: (0, i, 0, 0, 0)),
-            pl.BlockSpec((19, NZ, LANES), lambda i: (0, 0, 0)),
-        ],
-        out_specs=(out_block,) * 4,
+        in_specs=[vmem, vmem],
+        out_specs=(hbm,) * 4,
+        scratch_shapes=[pltpu.VMEM((4,) + block, F32), pltpu.SemaphoreType.DMA((4, NX // PART))],
+        compiler_params=pltpu.CompilerParams(vmem_limit_bytes=8 * 2**20),
         name="combine",
     )(basis, coefs)
 

time: 53 us -> 50.3 us (0.949)
  Pallas kernels: 52.1 us -> 49.5 us
    pallas_call x2, Pallas kernels: 52.1 us -> 49.5 us  [the longest x1 48.4 us: shards(): pl.pallas_call(main_kernel, out_shape=(pltpu.VMEM((6,) + inner, F32), plt...]
where the time goes in v2:
time: 50.3 us; the launch traced here: 50.1 us
  Pallas kernels  49.5 us (98%)
  between operations  0.64 us (1%)
    pallas_call x1, Pallas kernels, shards(): pl.pallas_call(main_kernel, out_shape=(pltpu.VMEM((6,) + inner, F32), plt...  48.4 us
    pallas_call x1, Pallas kernels, shards(): pl.pallas_call(combine_kernel, out_shape=(jax.ShapeDtypeStruct(block, F32...  1.05 us

profile of v2, /device:TPU:1, one launch (start us, length us, event | category | flops | bytes accessed | tf_op | source)
XLA Modules:
  0.0 50.1 jit_solution(10310551588400047606)
XLA Ops:
  0.6 48.4 %basis_and_sums.1 = (f32[6,24,2,8,128]{4,3,2,1,0:T(8,128)S(1)}, f32[19,8,128]{2,1,0:T(8,128)S(1)}) custom-call(f32[24,8,256]{2,1,0:T(8,128)} %b_hbm.1, f32[24,8,256]{2,1,0:T(8,128)} %k_hbm.1), custom_call_target="tpu_custom_call" | custom-call | tf_op jit(solution)/shard_map/basis_and_sums/pallas_call | solution.py:446
  49.0 1.1 %combine.1 = (f32[24,8,256]{2,1,0:T(8,128)}, f32[24,8,256]{2,1,0:T(8,128)}, f32[24,8,256]{2,1,0:T(8,128)}, f32[24,8,256]{2,1,0:T(8,128)}) custom-call(f32[6,24,2,8,128]{4,3,2,1,0:T(8,128)S(1)} %get-tuple-element.6.w_ref, f32[19,8,128]{2,1,0:T(8,128)S(1)} %get-tuple-element.7.coef_ref), custom_call_target="tpu_custom_call" | custom-call | tf_op jit(solution)/shard_map/combine/pallas_call | solution.py:477

commit v3 on v2

v3 whole, which is shorter than its diff:
```python
import functools

import jax
import jax.numpy as jnp
from jax import lax
from jax.experimental import pallas as pl
from jax.experimental.pallas import tpu as pltpu
from jax.sharding import PartitionSpec as P

MESH = pl.DeviceIdType.MESH
F32 = jnp.float32
NX, NZ, NY = 24, 8, 256
LANES = 128
PART = 12
GROUP = 32
GRAM = ((0, 0), (0, 1), (0, 2), (0, 3), (1, 1), (1, 2), (1, 3), (2, 2), (2, 3), (3, 3), (3, 4))


def shifted(axis, step):
    count = lax.axis_size(axis)
    return {axis: lax.rem(lax.axis_index(axis) + (step + count), count)}


def ring(step, count):
    return min(step % count, (-step) % count)


def group_line():
    lines = lax.axis_size("gx")
    gx, gz = lax.axis_index("gx"), lax.axis_index("gz")
    core = lax.rem(gz, 2)
    offsets = [(d, c) for d in range(lines) for c in range(2) if (d, c) != (0, 0)]
    offsets.sort(key=lambda o: -(2 * ring(o[0], lines) + o[1]))
    peers = [
        {"gx": lax.rem(gx + d, lines), "gz": gz - core + lax.rem(core + c, 2)} for d, c in offsets
    ]
    return gx * 2 + core, 2 * lines, peers


def group_plane():
    wide, deep = lax.axis_size("gy"), lax.axis_size("gz") // 2
    gy, gz = lax.axis_index("gy"), lax.axis_index("gz")
    offsets = [(d, e) for d in range(deep) for e in range(wide) if (d, e) != (0, 0)]
    offsets.sort(key=lambda o: -(ring(o[0], deep) + ring(o[1], wide)))
    peers = [
        {"gy": lax.rem(gy + e, wide), "gz": lax.rem(gz + 2 * d, 2 * deep)} for d, e in offsets
    ]
    return (gz // 2) * wide + gy, wide * deep, peers


def full(value):
    return jnp.broadcast_to(value, (NZ, LANES))


def total(value):
    return jnp.sum(jnp.sum(value, axis=0, keepdims=True), axis=1, keepdims=True)


def to_row(values):
    lane = lax.broadcasted_iota(jnp.int32, (1, LANES), 1)
    row = jnp.zeros((1, LANES), F32)
    for at, value in enumerate(values):
        row = jnp.where(lane == at, jnp.broadcast_to(total(value), (1, LANES)), row)
    return row


def solve(gram, c, s2):
    zero = jnp.zeros_like(c)
    one = jnp.ones_like(c)

    def g(i, j):
        return gram[(min(i, j), max(i, j))]

    gram = dict(gram)
    gram[(0, 4)] = g(1, 3) - s2 * g(0, 2)
    gram[(1, 4)] = g(2, 3) + s2 * (g(0, 3) - g(1, 2))
    gram[(2, 4)] = g(3, 3) + s2 * (g(1, 3) - g(2, 2))

    def image(a, top):
        out = []
        for i in range(top + 2):
            term = None
            if i <= top:
                term = c * a[i]
            if i >= 1:
                term = a[i - 1] if term is None else term + a[i - 1]
            if i + 1 <= top:
                term = term + s2 * a[i + 1]
            out.append(term)
        return out

    energy = {}
    for i in range(4):
        for j in range(i, 4):
            term = g(i, j + 1) + c * g(i, j)
            if j >= 1:
                term = term + s2 * g(i, j - 1)
            energy[(i, j)] = term

    def form(matrix, a, top):
        out = None
        for i in range(top + 1):
            part = matrix[(i, i)] * a[i]
            for j in range(i + 1, top + 1):
                part = part + (matrix[(i, j)] * 2.0) * a[j]
            out = a[i] * part if out is None else out + a[i] * part
        return out

    rho, way, answer = [one], [], []
    prior_norm = prior_step = None
    for turn in range(4):
        norm_now = form(gram, rho, turn)
        inner = form(energy, rho, turn)
        if turn == 0:
            step = norm_now / inner
            way = list(rho)
        else:
            ratio = norm_now / prior_norm
            step = norm_now / (inner - ratio * norm_now / prior_step)
            way = [rho[i] + ratio * way[i] if i < turn else rho[i] for i in range(turn + 1)]
        answer = [answer[i] + step * way[i] if i < turn else step * way[i] for i in range(turn + 1)]
        moved = image(way, turn)
        rho = [rho[i] - step * moved[i] if i <= turn else zero - step * moved[i] for i in range(turn + 2)]
        prior_norm, prior_step = norm_now, step
    third = image(rho[:4], 3)
    return answer, rho, third + [rho[4]], way


def main_kernel(b_hbm, k_hbm, w_ref, coef_ref,
                V, CX, CZL, CZH, CYL, CYH, GX, GZ, GY, ZS, ZR, YS, YR, XZ, ZY, XY, RS, RA, RB,
                copy_sem, halo_send, halo_recv, red_send, red_recv):
    gx, gy, gz = lax.axis_index("gx"), lax.axis_index("gy"), lax.axis_index("gz")
    core = lax.rem(gz, 2)
    rank_a, count_a, peers_a = group_line()
    rank_b, count_b, peers_b = group_plane()
    across = {"gz": lax.rem(gz + 2 * core - 1 + lax.axis_size("gz"), lax.axis_size("gz"))}
    pairs = (("gx", "gz"), ("gz", "gy"), ("gx", "gy"))
    slots = (0, 1)
    target, inside = {}, {}
    for axis, at in (("gx", gx), ("gy", gy), ("gz", gz)):
        for slot in slots:
            target[(axis, slot)] = shifted(axis, 1 - 2 * slot)
        inside[(axis, 0)], inside[(axis, 1)] = at > 0, at < lax.axis_size(axis) - 1
    corners = [(p, i, q, j) for p, q in pairs for i in slots for j in slots]
    for p, i, q, j in corners:
        target[(p, i, q, j)] = {**target[(p, i)], **target[(q, j)]}
        inside[(p, i, q, j)] = jnp.logical_and(inside[(p, i)], inside[(q, j)])

    loads = []
    for half in (0, 1):
        at = slice(half * LANES, (half + 1) * LANES)
        for what, ref in ((1, b_hbm), (0, k_hbm)):
            loads.append(pltpu.make_async_copy(ref.at[:, :, at], V.at[what, 2:NX + 2, half], copy_sem.at[what, half]))
    for load in loads:
        load.start()

    barrier = pltpu.get_barrier_semaphore()
    greeted = peers_b + peers_a + [target[corner] for corner in corners] + [across]
    for peer in greeted:
        pl.semaphore_signal(barrier, inc=1, device_id=peer, device_id_type=MESH)

    lane = lax.broadcasted_iota(jnp.int32, (NZ, LANES), 1)
    row = lax.broadcasted_iota(jnp.int32, (NZ, LANES), 0)
    lane_x = lax.broadcasted_iota(jnp.int32, (NX, LANES), 1)
    row_x = lax.broadcasted_iota(jnp.int32, (NX, LANES), 0)
    blank = jnp.zeros((NZ, LANES), F32)
    everything = []

    def faces():
        return [("gz", 0), ("gz", 1)], [("gx", 0), ("gx", 1), ("gy", 0), ("gy", 1)]

    def start_halo(phase, first, count, depth):
        what = pl.ds(first, count)
        ends = {}
        for slot in slots:
            low = NX + 2 - depth if slot == 0 else 2
            ghost = 2 - depth if slot == 0 else NX + 2
            ends[("gx", slot)] = V.at[what, low:low + depth], V.at[what, ghost:ghost + depth]
            ends[("gz", slot)] = ZS.at[what, slot, 0:depth], ZR.at[what, slot, 0:depth]
            ends[("gy", slot)] = YS.at[phase, slot], YR.at[phase, slot]
        for i in slots if depth == 2 else ():
            for j in slots:
                at = NX - 1 if i == 0 else 0
                ends[("gx", i, "gz", j)] = ZS.at[what, j, 0, :, at:at + 1], XZ.at[what, i, j, :, at:at + 1]
                at = NZ - 1 if i == 0 else 0
                ends[("gz", i, "gy", j)] = YS.at[phase, j, at:at + 1], ZY.at[phase, i, j, at:at + 1]
                ends[("gx", i, "gy", j)] = YS.at[phase, j], XY.at[phase, i, j]
        head, tail = faces()
        order = head + (corners if depth == 2 else []) + tail
        sent = []
        for at, name in enumerate(order):
            src, dst = ends[name]
            sent.append(pltpu.make_async_remote_copy(
                src_ref=src, dst_ref=dst, send_sem=halo_send.at[phase, at], recv_sem=halo_recv.at[phase, at],
                device_id=target[name], device_id_type=MESH,
            ))
            sent[-1].start()
        everything.extend(sent)
        return sent

    def keep(flag, value):
        return jnp.where(flag, value, jnp.zeros_like(value))

    def end_halo(sent, first, count, depth):
        for copy in sent:
            copy.wait_recv()
        for what in range(first, first + count):
            for slot in slots:
                for layer in range(depth):
                    at = 1 - layer if slot == 0 else NX + 2 + layer
                    V[what, at] = keep(inside[("gx", slot)], V[what, at])
                    ZR[what, slot, layer] = keep(inside[("gz", slot)], ZR[what, slot, layer])

    def tiles(ref, *at):
        return ref[(*at, 0)], ref[(*at, 1)]

    def put(ref, at, pair):
        ref[(*at, 0)], ref[(*at, 1)] = pair

    def turned(value, by):
        return pltpu.roll(value, by % LANES, 1)

    def lanes_down(pair, packed, x):
        first, second = turned(pair[0], 1), turned(pair[1], 1)
        edge = pltpu.roll(packed, lax.rem(LANES - x, LANES), 1)
        return jnp.where(lane == 0, edge, first), jnp.where(lane == 0, first, second)

    def lanes_up(pair, packed, x):
        first, second = turned(pair[0], -1), turned(pair[1], -1)
        edge = pltpu.roll(packed, LANES - 1 - x, 1)
        return jnp.where(lane == LANES - 1, second, first), jnp.where(lane == LANES - 1, edge, second)

    def rows_down(pair, halo):
        return tuple(jnp.where(row == 0, full(h), pltpu.roll(p, 1, 0)) for p, h in zip(pair, halo))

    def rows_up(pair, halo):
        return tuple(jnp.where(row == NZ - 1, full(h), pltpu.roll(p, NZ - 1, 0)) for p, h in zip(pair, halo))

    def halo_row(what, slot, x):
        return tuple(ZR[what, slot, 0, half, pl.ds(x, 1), :] for half in (0, 1))

    def loop(body, carry):
        return lax.fori_loop(0, NX, body, carry, unroll=True)

    def pack_rows(what, depth):
        flat = V.at[what].reshape((NX + 4) * 2 * NZ, LANES)
        for slot in slots:
            for layer in range(depth):
                at = NZ - 1 - layer if slot == 0 else layer
                for half in (0, 1):
                    ZS[what, slot, layer, half] = flat[pl.ds((4 + half) * NZ + at, NX, stride=2 * NZ), :]

    def pack_lanes(pair, packed, x, start, depth):
        up, down = packed
        for layer in range(depth):
            at = start + GROUP * layer
            here = lane == x + at
            up = jnp.where(here, pltpu.roll(pair[1], lax.rem(x + at + 1 + layer, LANES), 1), up)
            down = jnp.where(here, pltpu.roll(pair[0], lax.rem(x + at + LANES - layer, LANES), 1), down)
        return up, down

    def y_tile(phase, slot, start):
        return turned(keep(inside[("gy", slot)], YR[phase, slot]), -start)

    def ghosts_x(phase, what, start, slot):
        at = 1 if slot == 0 else NX + 2
        x = NX - 1 if slot == 0 else 0
        here = tiles(V, what, at)
        lines = [
            tuple(keep(inside[("gx", slot, "gz", j)], XZ[what, slot, j, half, x:x + 1, :]) for half in (0, 1))
            for j in slots
        ]
        sides = [turned(keep(inside[("gx", slot, "gy", j)], XY[phase, slot, j]), -start) for j in slots]
        return here, (
            tiles(V, what, at - 1), tiles(V, what, at + 1), rows_down(here, lines[0]), rows_up(here, lines[1]),
            lanes_down(here, sides[0], x), lanes_up(here, sides[1], x),
        )

    def ghosts_z(phase, what, start, slot):
        here, outer, inner = tiles(ZR, what, slot, 0), tiles(ZR, what, slot, 1), tiles(ZS, what, 1 - slot, 0)

        def line(i, half):
            at = NX - 1 if i == 0 else 0
            value = keep(inside[("gx", i, "gz", slot)], XZ[what, i, slot, half, at:at + 1, :])
            return jnp.broadcast_to(value, (NX, LANES))

        def column(j):
            at = NZ - 1 if slot == 0 else 0
            value = keep(inside[("gz", slot, "gy", j)], ZY[phase, slot, j, at:at + 1, :])
            spread = jnp.where(lane_x == row_x + start, jnp.broadcast_to(value, (NX, LANES)), 0.0)
            return jnp.broadcast_to(jnp.sum(spread, axis=1, keepdims=True), (NX, LANES))

        before = tuple(jnp.where(row_x == 0, line(0, half), pltpu.roll(here[half], 1, 0)) for half in (0, 1))
        after = tuple(jnp.where(row_x == NX - 1, line(1, half), pltpu.roll(here[half], NX - 1, 0)) for half in (0, 1))
        down = [turned(here[half], 1) for half in (0, 1)]
        up = [turned(here[half], -1) for half in (0, 1)]
        left = jnp.where(lane_x == 0, column(0), down[0]), jnp.where(lane_x == 0, down[0], down[1])
        last = lane_x == LANES - 1
        right = jnp.where(last, up[1], up[0]), jnp.where(last, column(1), up[1])
        return here, (before, after, outer, inner, left, right)

    def ghosts_y(phase, what, start, slot):
        here = y_tile(phase, slot, start)
        outer = y_tile(phase, slot, start + GROUP)
        inner = turned(YS[phase, 1 - slot], -start)
        lines, sides = [], []
        for i in slots:
            at = NZ - 1 if i == 0 else 0
            value = keep(inside[("gz", i, "gy", slot)], ZY[phase, i, slot, at:at + 1, :])
            lines.append(turned(full(value), -start))
            value = turned(keep(inside[("gx", i, "gy", slot)], XY[phase, i, slot]), -start)
            sides.append(turned(value, 1 - NX if i == 0 else NX - 1))
        before = jnp.where(lane == 0, sides[0], turned(here, 1))
        after = jnp.where(lane == NX - 1, sides[1], turned(here, -1))
        low = jnp.where(row == 0, lines[0], pltpu.roll(here, 1, 0))
        high = jnp.where(row == NZ - 1, lines[1], pltpu.roll(here, NZ - 1, 0))
        return (here,), ((before,), (after,), (low,), (high,), (outer,), (inner,))

    regions = ((ghosts_x, GX, "gx"), (ghosts_z, GZ, "gz"), (ghosts_y, GY, "gy"))

    def ghost_conds():
        for find, ref, _ in regions:
            for slot in slots:
                here, others = find(0, 0, 0, slot)
                for at, other in enumerate(others):
                    for part, (a, b) in enumerate(zip(here, other)):
                        ref[slot, at, part] = (a + b) * 0.5

    def ghost_image(phase, what, start):
        sides = []
        for find, ref, axis in regions:
            for slot in slots:
                here, others = find(phase, what, start, slot)
                out = [None] * len(here)
                for at, other in enumerate(others):
                    for part, (a, b) in enumerate(zip(here, other)):
                        term = ref[slot, at, part] * (a - b)
                        out[part] = term if out[part] is None else out[part] + term
                out = tuple(keep(inside[(axis, slot)], value) for value in out)
                if axis == "gx":
                    put(V, (what + 1, 1 if slot == 0 else NX + 2), out)
                elif axis == "gz":
                    put(ZR, (what + 1, slot, 0), out)
                else:
                    sides.append(out[0])
        return sides

    for load in loads:
        load.wait()

    def pack_both(x, packed):
        for what in (0, 1):
            packed = pack_lanes(tiles(V, what, x + 2), packed, x, 2 * GROUP * what, 2)
        return packed

    packed = loop(pack_both, (blank, blank))
    YS[0, 0], YS[0, 1] = packed
    for what in (0, 1):
        pack_rows(what, 2)
    pl.semaphore_wait(barrier, len(greeted))
    sent = start_halo(0, 0, 2, 2)

    def own_part(x, state):
        before, sums = state
        here, coeff = tiles(V, 1, x + 2), tiles(V, 0, x + 2)
        after = tuple(
            (a + b) * 0.5 * (n - h)
            for a, b, n, h in zip(coeff, tiles(V, 0, x + 3), tiles(V, 1, x + 3), here)
        )
        after = tuple(jnp.where(x < NX - 1, value, 0.0) for value in after)
        out = tuple(a - b for a, b in zip(before, after))
        for shift, edge in ((1, 0), (NZ - 1, NZ - 1)):
            out = tuple(
                o + jnp.where(row == edge, 0.0, (k + pltpu.roll(k, shift, 0)) * 0.5 * (h - pltpu.roll(h, shift, 0)))
                for o, k, h in zip(out, coeff, here)
            )
        for shift, edge, end in ((1, 0, 0), (-1, LANES - 1, 1)):
            k_turn, h_turn = [turned(k, shift) for k in coeff], [turned(h, shift) for h in here]
            terms = []
            for half in (0, 1):
                k_next = k_turn[half] if half == end else jnp.where(lane == edge, k_turn[1 - half], k_turn[half])
                h_next = h_turn[half] if half == end else jnp.where(lane == edge, h_turn[1 - half], h_turn[half])
                term = (coeff[half] + k_next) * 0.5 * (here[half] - h_next)
                terms.append(jnp.where(lane == edge, 0.0, term) if half == end else term)
            out = tuple(o + t for o, t in zip(out, terms))
        sums = (
            sums[0] + here[0] * here[0] + here[1] * here[1],
            sums[1] + here[0] * out[0] + here[1] * out[1],
            sums[2] + out[0] * out[0] + out[1] * out[1],
        )
        return after, sums

    def send_sum(at, which, values):
        rank, count, peers, ref = (
            (rank_a, count_a, peers_a, RA) if which == 0 else (rank_b, count_b, peers_b, RB)
        )
        RS[at, which] = values
        for peer in peers:
            pltpu.make_async_remote_copy(
                src_ref=RS.at[at, which], dst_ref=ref.at[at, rank], send_sem=red_send.at[at, which],
                recv_sem=red_recv.at[at, which], device_id=peer, device_id_type=MESH,
            ).start()
        ref[at, rank] = values
        whole = ref.at[at, 0:count - 1]
        waits = pltpu.make_async_remote_copy(
            src_ref=whole, dst_ref=whole, send_sem=red_send.at[at, which], recv_sem=red_recv.at[at, which],
            device_id=peers[0], device_id_type=MESH,
        )
        everything.append(waits)
        return waits

    def end_sum(at, which, waits):
        waits.wait_recv()
        return jnp.sum((RA if which == 0 else RB)[at], axis=0)

    sums = loop(own_part, ((blank, blank), (blank, blank, blank)))[1]
    first_a = send_sum(0, 0, to_row(sums))
    end_halo(sent, 0, 2, 2)

    put(CX, (0,), tuple((a + b) * 0.5 for a, b in zip(tiles(V, 0, 1), tiles(V, 0, 2))))
    edges_k = [y_tile(0, slot, 0) for slot in slots]

    def conds(x, carry):
        here = tiles(V, 0, x + 2)
        for ref, other in (
            (CX.at[x + 1], tiles(V, 0, x + 3)),
            (CZL.at[x], rows_down(here, halo_row(0, 0, x))),
            (CZH.at[x], rows_up(here, halo_row(0, 1, x))),
            (CYL.at[x], lanes_down(here, edges_k[0], x)),
            (CYH.at[x], lanes_up(here, edges_k[1], x)),
        ):
            put(ref, (), tuple((a + b) * 0.5 for a, b in zip(here, other)))
        return carry

    loop(conds, 0)
    ghost_conds()

    def stencil(what, edges, write, carry):
        def body(x, state):
            before, inner = state
            here = tiles(V, what, x + 2)
            after = tuple(c * (n - h) for c, n, h in zip(tiles(CX, x + 1), tiles(V, what, x + 3), here))
            out = tuple(a - b for a, b in zip(before, after))
            for cond, other in (
                (CZL, rows_down(here, halo_row(what, 0, x))),
                (CZH, rows_up(here, halo_row(what, 1, x))),
                (CYL, lanes_down(here, edges[0], x)),
                (CYH, lanes_up(here, edges[1], x)),
            ):
                out = tuple(o + c * (h - n) for o, c, h, n in zip(out, tiles(cond, x), here, other))
            return after, write(x, out, inner)

        first = tuple(c * (n - h) for c, n, h in zip(tiles(CX, 0), tiles(V, what, 2), tiles(V, what, 1)))
        return loop(body, (first, carry))[1]

    def advance(what, edges, depth):
        def write(x, out, packed):
            put(V, (what + 1, x + 2), out)
            return pack_lanes(out, packed, x, 0, depth)

        return stencil(what, edges, write, (blank, blank))

    advance(1, [y_tile(0, slot, 2 * GROUP) for slot in slots], 0)
    edges = ghost_image(0, 1, 2 * GROUP)
    YS[1, 0], YS[1, 1] = advance(2, edges, 2)
    pack_rows(3, 2)
    sent = start_halo(1, 3, 1, 2)
    first_b = send_sum(0, 1, end_sum(0, 0, first_a))
    end_halo(sent, 3, 1, 2)
    advance(3, [y_tile(1, slot, 0) for slot in slots], 0)
    edges = ghost_image(1, 3, 0)
    advance(4, edges, 0)

    moments = end_sum(0, 1, first_b)
    m0, m1, m2 = (full(moments[:, at:at + 1]) for at in range(3))
    c = m1 / m0
    s2 = jnp.maximum(m2 / m0 - c * c, 0.0)

    def basis(x, carry):
        packed, sums = carry
        powers = [tiles(V, at, x + 2) for at in range(1, 6)]
        fields = []
        for half in (0, 1):
            v = [power[half] for power in powers]
            one = [v[at + 1] - c * v[at] for at in range(4)]
            two = [one[at + 1] - c * one[at] - s2 * v[at] for at in range(3)]
            three = [two[at + 1] - c * two[at] - s2 * one[at] for at in range(2)]
            four = three[1] - c * three[0] - s2 * two[0]
            fields.append((v[0], one[0], two[0], three[0], four))
        for at in range(5):
            put(w_ref, (at, x), (fields[0][at], fields[1][at]))
        last = (fields[0][4], fields[1][4])
        put(V, (5, x + 2), last)
        sums = tuple(
            s + fields[0][i] * fields[0][j] + fields[1][i] * fields[1][j] for s, (i, j) in zip(sums, GRAM)
        )
        return pack_lanes(last, packed, x, 0, 1), sums

    packed, sums = loop(basis, ((blank, blank), (blank,) * len(GRAM)))
    second_a = send_sum(1, 0, to_row(sums))
    YS[2, 0], YS[2, 1] = packed
    pack_rows(5, 1)
    sent = start_halo(2, 5, 1, 1)
    end_halo(sent, 5, 1, 1)

    def last_image(x, out, carry):
        put(w_ref, (5, x), out)
        return carry

    stencil(5, [y_tile(2, slot, 0) for slot in slots], last_image, 0)
    second_b = send_sum(1, 1, end_sum(1, 0, second_a))
    entries = end_sum(1, 1, second_b)
    gram = {pair: full(entries[:, at:at + 1]) for at, pair in enumerate(GRAM)}
    at = 0
    for part in solve(gram, c, s2):
        for value in part:
            coef_ref[at] = value
            at += 1

    for copy in everything:
        copy.wait_send()


def combine_kernel(w_ref, coef_ref, solution_ref, residual_ref, image_ref, direction_ref, held, sems):
    refs = (solution_ref, residual_ref, image_ref, direction_ref)
    copies = []
    for part in range(NX // PART):
        for x in range(part * PART, (part + 1) * PART):
            for half in (0, 1):
                at = slice(half * LANES, (half + 1) * LANES)
                w = [w_ref[i, x, half] for i in range(6)]
                start = 0
                for which, count in enumerate((4, 5, 6, 4)):
                    out = coef_ref[start] * w[0]
                    for i in range(1, count):
                        out = out + coef_ref[start + i] * w[i]
                    held[which, x, :, at] = out
                    start += count
        rows = pl.ds(part * PART, PART)
        for which, ref in enumerate(refs):
            copies.append(pltpu.make_async_copy(held.at[which, rows], ref.at[rows], sems.at[which, part]))
            copies[-1].start()
    for copy in copies:
        copy.wait()


def shards(right_side, kappa):
    line, plane = 2 * lax.axis_size("gx"), lax.axis_size("gy") * lax.axis_size("gz") // 2
    hbm = pl.BlockSpec(memory_space=pltpu.MemorySpace.HBM)
    vmem = pl.BlockSpec(memory_space=pltpu.VMEM)
    block, inner = (NX, NZ, NY), (NX, 2, NZ, LANES)
    basis, coefs = pl.pallas_call(
        main_kernel,
        out_shape=(pltpu.VMEM((6,) + inner, F32), pltpu.VMEM((19, NZ, LANES), F32)),
        in_specs=[hbm, hbm],
        out_specs=(vmem, vmem),
        scratch_shapes=[
            pltpu.VMEM((6, NX + 4, 2, NZ, LANES), F32),
            pltpu.VMEM((NX + 1, 2, NZ, LANES), F32),
            pltpu.VMEM(inner, F32),
            pltpu.VMEM(inner, F32),
            pltpu.VMEM(inner, F32),
            pltpu.VMEM(inner, F32),
            pltpu.VMEM((2, 6, 2, NZ, LANES), F32),
            pltpu.VMEM((2, 6, 2, NX, LANES), F32),
            pltpu.VMEM((2, 6, 1, NZ, LANES), F32),
            pltpu.VMEM((6, 2, 2, 2, NX, LANES), F32),
            pltpu.VMEM((6, 2, 2, 2, NX, LANES), F32),
            pltpu.VMEM((3, 2, NZ, LANES), F32),
            pltpu.VMEM((3, 2, NZ, LANES), F32),
            pltpu.VMEM((4, 2, 2, 2, NX, LANES), F32),
            pltpu.VMEM((2, 2, 2, NZ, LANES), F32),
            pltpu.VMEM((2, 2, 2, NZ, LANES), F32),
            pltpu.VMEM((2, 2, 1, LANES), F32),
            pltpu.VMEM((2, line, 1, LANES), F32),
            pltpu.VMEM((2, plane, 1, LANES), F32),
            pltpu.SemaphoreType.DMA((2, 2)),
            pltpu.SemaphoreType.DMA((3, 18)),
            pltpu.SemaphoreType.DMA((3, 18)),
            pltpu.SemaphoreType.DMA((2, 2)),
            pltpu.SemaphoreType.DMA((2, 2)),
        ],
        compiler_params=pltpu.CompilerParams(collective_id=0, has_side_effects=True, vmem_limit_bytes=60 * 2**20),
        name="basis_and_sums",
    )(right_side, kappa)
    return pl.pallas_call(
        combine_kernel,
        out_shape=(jax.ShapeDtypeStruct(block, F32),) * 4,
        in_specs=[vmem, vmem],
        out_specs=(hbm,) * 4,
        scratch_shapes=[pltpu.VMEM((4,) + block, F32), pltpu.SemaphoreType.DMA((4, NX // PART))],
        compiler_params=pltpu.CompilerParams(vmem_limit_bytes=8 * 2**20),
        name="combine",
    )(basis, coefs)


def solution(mesh):
    placed = P("gx", "gz", "gy")
    return jax.shard_map(
        shards,
        mesh=mesh,
        in_specs=(placed, placed),
        out_specs=(placed,) * 4,
        check_vma=False,
    )
```

time: 50.3 us -> 46.7 us (0.928)
  Pallas kernels: 49.5 us -> 45.9 us
    pallas_call x1, Pallas kernels: 48.4 us -> 44.9 us  [shards(): pl.pallas_call(main_kernel, out_shape=(pltpu.VMEM((6,) + inner, F32), plt...]
where the time goes in v3:
time: 46.7 us; the launch traced here: 46.6 us
  Pallas kernels  45.9 us (98%)
  between operations  0.64 us (1%)
    pallas_call x1, Pallas kernels, shards(): pl.pallas_call(main_kernel, out_shape=(pltpu.VMEM((6,) + inner, F32), plt...  44.9 us
    pallas_call x1, Pallas kernels, shards(): pl.pallas_call(combine_kernel, out_shape=(jax.ShapeDtypeStruct(block, F32...  1.05 us

profile of v3, /device:TPU:1, one launch (start us, length us, event | category | flops | bytes accessed | tf_op | source)
XLA Modules:
  0.0 46.6 jit_solution(15213798452888154369)
XLA Ops:
  0.6 44.9 %basis_and_sums.1 = (f32[6,24,2,8,128]{4,3,2,1,0:T(8,128)S(1)}, f32[19,8,128]{2,1,0:T(8,128)S(1)}) custom-call(f32[24,8,256]{2,1,0:T(8,128)} %b_hbm.1, f32[24,8,256]{2,1,0:T(8,128)} %k_hbm.1), custom_call_target="tpu_custom_call" | custom-call | tf_op jit(solution)/shard_map/basis_and_sums/pallas_call | solution.py:552
  45.5 1.1 %combine.1 = (f32[24,8,256]{2,1,0:T(8,128)}, f32[24,8,256]{2,1,0:T(8,128)}, f32[24,8,256]{2,1,0:T(8,128)}, f32[24,8,256]{2,1,0:T(8,128)}) custom-call(f32[6,24,2,8,128]{4,3,2,1,0:T(8,128)S(1)} %get-tuple-element.6.w_ref, f32[19,8,128]{2,1,0:T(8,128)S(1)} %get-tuple-element.7.coef_ref), custom_call_target="tpu_custom_call" | custom-call | tf_op jit(solution)/shard_map/combine/pallas_call | solution.py:586

commit v4 on v3

--- a/solution.py
+++ b/solution.py
@@ -13,6 +13,7 @@
 LANES = 128
 PART = 12
 GROUP = 32
+FAR = 16
 GRAM = ((0, 0), (0, 1), (0, 2), (0, 3), (1, 1), (1, 2), (1, 3), (2, 2), (2, 3), (3, 3), (3, 4))
 
 
@@ -32,7 +33,8 @@
     offsets = [(d, c) for d in range(lines) for c in range(2) if (d, c) != (0, 0)]
     offsets.sort(key=lambda o: -(2 * ring(o[0], lines) + o[1]))
     peers = [
-        {"gx": lax.rem(gx + d, lines), "gz": gz - core + lax.rem(core + c, 2)} for d, c in offsets
+        (ring(d, lines), {"gx": lax.rem(gx + d, lines), "gz": gz - core + lax.rem(core + c, 2)})
+        for d, c in offsets
     ]
     return gx * 2 + core, 2 * lines, peers
 
@@ -43,7 +45,8 @@
     offsets = [(d, e) for d in range(deep) for e in range(wide) if (d, e) != (0, 0)]
     offsets.sort(key=lambda o: -(ring(o[0], deep) + ring(o[1], wide)))
     peers = [
-        {"gy": lax.rem(gy + e, wide), "gz": lax.rem(gz + 2 * d, 2 * deep)} for d, e in offsets
+        (ring(d, deep) + ring(e, wide), {"gy": lax.rem(gy + e, wide), "gz": lax.rem(gz + 2 * d, 2 * deep)})
+        for d, e in offsets
     ]
     return (gz // 2) * wide + gy, wide * deep, peers
 
@@ -146,6 +149,15 @@
         target[(p, i, q, j)] = {**target[(p, i)], **target[(q, j)]}
         inside[(p, i, q, j)] = jnp.logical_and(inside[(p, i)], inside[(q, j)])
 
+    barrier = pltpu.get_barrier_semaphore()
+    greeted = peers_a + peers_b + [(2, target[corner]) for corner in corners] + [(1, across)]
+    greeted.sort(key=lambda pair: -pair[0])
+
+    def greet(some):
+        for _, peer in some:
+            pl.semaphore_signal(barrier, inc=1, device_id=peer, device_id_type=MESH)
+
+    greet(greeted[:FAR])
     loads = []
     for half in (0, 1):
         at = slice(half * LANES, (half + 1) * LANES)
@@ -153,11 +165,7 @@
             loads.append(pltpu.make_async_copy(ref.at[:, :, at], V.at[what, 2:NX + 2, half], copy_sem.at[what, half]))
     for load in loads:
         load.start()
-
-    barrier = pltpu.get_barrier_semaphore()
-    greeted = peers_b + peers_a + [target[corner] for corner in corners] + [across]
-    for peer in greeted:
-        pl.semaphore_signal(barrier, inc=1, device_id=peer, device_id_type=MESH)
+    greet(greeted[FAR:])
 
     lane = lax.broadcasted_iota(jnp.int32, (NZ, LANES), 1)
     row = lax.broadcasted_iota(jnp.int32, (NZ, LANES), 0)
@@ -357,9 +365,6 @@
     YS[0, 0], YS[0, 1] = packed
     for what in (0, 1):
         pack_rows(what, 2)
-    pl.semaphore_wait(barrier, len(greeted))
-    sent = start_halo(0, 0, 2, 2)
-
     def own_part(x, state):
         before, sums = state
         here, coeff = tiles(V, 1, x + 2), tiles(V, 0, x + 2)
@@ -395,7 +400,7 @@
             (rank_a, count_a, peers_a, RA) if which == 0 else (rank_b, count_b, peers_b, RB)
         )
         RS[at, which] = values
-        for peer in peers:
+        for _, peer in peers:
             pltpu.make_async_remote_copy(
                 src_ref=RS.at[at, which], dst_ref=ref.at[at, rank], send_sem=red_send.at[at, which],
                 recv_sem=red_recv.at[at, which], device_id=peer, device_id_type=MESH,
@@ -404,7 +409,7 @@
         whole = ref.at[at, 0:count - 1]
         waits = pltpu.make_async_remote_copy(
             src_ref=whole, dst_ref=whole, send_sem=red_send.at[at, which], recv_sem=red_recv.at[at, which],
-            device_id=peers[0], device_id_type=MESH,
+            device_id=peers[0][1], device_id_type=MESH,
         )
         everything.append(waits)
         return waits
@@ -413,8 +418,10 @@
         waits.wait_recv()
         return jnp.sum((RA if which == 0 else RB)[at], axis=0)
 
-    sums = loop(own_part, ((blank, blank), (blank, blank, blank)))[1]
-    first_a = send_sum(0, 0, to_row(sums))
+    sums = to_row(loop(own_part, ((blank, blank), (blank, blank, blank)))[1])
+    pl.semaphore_wait(barrier, len(greeted))
+    first_a = send_sum(0, 0, sums)
+    sent = start_halo(0, 0, 2, 2)
     end_halo(sent, 0, 2, 2)
 
     put(CX, (0,), tuple((a + b) * 0.5 for a, b in zip(tiles(V, 0, 1), tiles(V, 0, 2))))
@@ -462,10 +469,10 @@
 
     advance(1, [y_tile(0, slot, 2 * GROUP) for slot in slots], 0)
     edges = ghost_image(0, 1, 2 * GROUP)
+    first_b = send_sum(0, 1, end_sum(0, 0, first_a))
     YS[1, 0], YS[1, 1] = advance(2, edges, 2)
     pack_rows(3, 2)
     sent = start_halo(1, 3, 1, 2)
-    first_b = send_sum(0, 1, end_sum(0, 0, first_a))
     end_halo(sent, 3, 1, 2)
     advance(3, [y_tile(1, slot, 0) for slot in slots], 0)
     edges = ghost_image(1, 3, 0)
@@ -509,6 +516,8 @@
 
     stencil(5, [y_tile(2, slot, 0) for slot in slots], last_image, 0)
     second_b = send_sum(1, 1, end_sum(1, 0, second_a))
+    for copy in everything[:-1]:
+        copy.wait_send()
     entries = end_sum(1, 1, second_b)
     gram = {pair: full(entries[:, at:at + 1]) for at, pair in enumerate(GRAM)}
     at = 0
@@ -517,8 +526,7 @@
             coef_ref[at] = value
             at += 1
 
-    for copy in everything:
-        copy.wait_send()
+    second_b.wait_send()
 
 
 def combine_kernel(w_ref, coef_ref, solution_ref, residual_ref, image_ref, direction_ref, held, sems):

time: 46.7 us -> 46.2 us (0.989)
  Pallas kernels: 45.9 us -> 45.4 us
    pallas_call x1, Pallas kernels: 44.9 us -> 44.3 us  [shards(): pl.pallas_call(main_kernel, out_shape=(pltpu.VMEM((6,) + inner, F32), plt...]
where the time goes in v4:
time: 46.2 us; the launch traced here: 46 us
  Pallas kernels  45.4 us (98%)
  between operations  0.64 us (1%)
    pallas_call x1, Pallas kernels, shards(): pl.pallas_call(main_kernel, out_shape=(pltpu.VMEM((6,) + inner, F32), plt...  44.3 us
    pallas_call x1, Pallas kernels, shards(): pl.pallas_call(combine_kernel, out_shape=(jax.ShapeDtypeStruct(block, F32...  1.05 us

profile of v4, /device:TPU:1, one launch (start us, length us, event | category | flops | bytes accessed | tf_op | source)
XLA Modules:
  0.0 46.0 jit_solution(4154027580880498621)
XLA Ops:
  0.6 44.3 %basis_and_sums.1 = (f32[6,24,2,8,128]{4,3,2,1,0:T(8,128)S(1)}, f32[19,8,128]{2,1,0:T(8,128)S(1)}) custom-call(f32[24,8,256]{2,1,0:T(8,128)} %b_hbm.1, f32[24,8,256]{2,1,0:T(8,128)} %k_hbm.1), custom_call_target="tpu_custom_call" | custom-call | tf_op jit(solution)/shard_map/basis_and_sums/pallas_call | solution.py:560
  45.0 1.1 %combine.1 = (f32[24,8,256]{2,1,0:T(8,128)}, f32[24,8,256]{2,1,0:T(8,128)}, f32[24,8,256]{2,1,0:T(8,128)}, f32[24,8,256]{2,1,0:T(8,128)}) custom-call(f32[6,24,2,8,128]{4,3,2,1,0:T(8,128)S(1)} %get-tuple-element.6.w_ref, f32[19,8,128]{2,1,0:T(8,128)S(1)} %get-tuple-element.7.coef_ref), custom_call_target="tpu_custom_call" | custom-call | tf_op jit(solution)/shard_map/combine/pallas_call | solution.py:594

commit v5 on v4

--- a/solution.py
+++ b/solution.py
@@ -11,7 +11,7 @@
 F32 = jnp.float32
 NX, NZ, NY = 24, 8, 256
 LANES = 128
-PART = 12
+PART = 6
 GROUP = 32
 FAR = 16
 GRAM = ((0, 0), (0, 1), (0, 2), (0, 3), (1, 1), (1, 2), (1, 3), (2, 2), (2, 3), (3, 3), (3, 4))
@@ -328,14 +328,17 @@
 
     def ghost_conds():
         for find, ref, _ in regions:
+            found = {}
             for slot in slots:
                 here, others = find(0, 0, 0, slot)
                 for at, other in enumerate(others):
                     for part, (a, b) in enumerate(zip(here, other)):
-                        ref[slot, at, part] = (a + b) * 0.5
+                        found[(slot, at, part)] = (a + b) * 0.5
+            for name, value in found.items():
+                ref[name] = value
 
     def ghost_image(phase, what, start):
-        sides = []
+        found, sides = [], []
         for find, ref, axis in regions:
             for slot in slots:
                 here, others = find(phase, what, start, slot)
@@ -346,11 +349,13 @@
                         out[part] = term if out[part] is None else out[part] + term
                 out = tuple(keep(inside[(axis, slot)], value) for value in out)
                 if axis == "gx":
-                    put(V, (what + 1, 1 if slot == 0 else NX + 2), out)
+                    found.append((V, (what + 1, 1 if slot == 0 else NX + 2), out))
                 elif axis == "gz":
-                    put(ZR, (what + 1, slot, 0), out)
+                    found.append((ZR, (what + 1, slot, 0), out))
                 else:
                     sides.append(out[0])
+        for item in found:
+            put(*item)
         return sides
 
     for load in loads:
@@ -367,10 +372,11 @@
         pack_rows(what, 2)
     def own_part(x, state):
         before, sums = state
+        above = jnp.minimum(x + 3, NX + 1)
         here, coeff = tiles(V, 1, x + 2), tiles(V, 0, x + 2)
         after = tuple(
             (a + b) * 0.5 * (n - h)
-            for a, b, n, h in zip(coeff, tiles(V, 0, x + 3), tiles(V, 1, x + 3), here)
+            for a, b, n, h in zip(coeff, tiles(V, 0, above), tiles(V, 1, above), here)
         )
         after = tuple(jnp.where(x < NX - 1, value, 0.0) for value in after)
         out = tuple(a - b for a, b in zip(before, after))

time: 46.2 us -> 46.2 us (level)
  no operation moved by 1% of the time
where the time goes in v5:
time: 46.2 us; the launch traced here: 46 us
  Pallas kernels  45.4 us (98%)
  between operations  0.64 us (1%)
    pallas_call x1, Pallas kernels, shards(): pl.pallas_call(main_kernel, out_shape=(pltpu.VMEM((6,) + inner, F32), plt...  44.3 us
    pallas_call x1, Pallas kernels, shards(): pl.pallas_call(combine_kernel, out_shape=(jax.ShapeDtypeStruct(block, F32...  1.06 us

profile of v5, /device:TPU:1, one launch (start us, length us, event | category | flops | bytes accessed | tf_op | source)
XLA Modules:
  0.0 46.0 jit_solution(1281788615138150245)
XLA Ops:
  0.6 44.3 %basis_and_sums.1 = (f32[6,24,2,8,128]{4,3,2,1,0:T(8,128)S(1)}, f32[19,8,128]{2,1,0:T(8,128)S(1)}) custom-call(f32[24,8,256]{2,1,0:T(8,128)} %b_hbm.1, f32[24,8,256]{2,1,0:T(8,128)} %k_hbm.1), custom_call_target="tpu_custom_call" | custom-call | tf_op jit(solution)/shard_map/basis_and_sums/pallas_call | solution.py:566
  45.0 1.1 %combine.1 = (f32[24,8,256]{2,1,0:T(8,128)}, f32[24,8,256]{2,1,0:T(8,128)}, f32[24,8,256]{2,1,0:T(8,128)}, f32[24,8,256]{2,1,0:T(8,128)}) custom-call(f32[6,24,2,8,128]{4,3,2,1,0:T(8,128)S(1)} %get-tuple-element.6.w_ref, f32[19,8,128]{2,1,0:T(8,128)S(1)} %get-tuple-element.7.coef_ref), custom_call_target="tpu_custom_call" | custom-call | tf_op jit(solution)/shard_map/combine/pallas_call | solution.py:600

commit v6 on v5

--- a/solution.py
+++ b/solution.py
@@ -489,8 +489,7 @@
     c = m1 / m0
     s2 = jnp.maximum(m2 / m0 - c * c, 0.0)
 
-    def basis(x, carry):
-        packed, sums = carry
+    def basis(x):
         powers = [tiles(V, at, x + 2) for at in range(1, 6)]
         fields = []
         for half in (0, 1):
@@ -500,18 +499,22 @@
             three = [two[at + 1] - c * two[at] - s2 * one[at] for at in range(2)]
             four = three[1] - c * three[0] - s2 * two[0]
             fields.append((v[0], one[0], two[0], three[0], four))
+        return fields
+
+    def products(x, sums):
+        low, high = basis(x)
+        return tuple(s + low[i] * low[j] + high[i] * high[j] for s, (i, j) in zip(sums, GRAM))
+
+    def keep_basis(x, packed):
+        low, high = basis(x)
         for at in range(5):
-            put(w_ref, (at, x), (fields[0][at], fields[1][at]))
-        last = (fields[0][4], fields[1][4])
+            put(w_ref, (at, x), (low[at], high[at]))
+        last = (low[4], high[4])
         put(V, (5, x + 2), last)
-        sums = tuple(
-            s + fields[0][i] * fields[0][j] + fields[1][i] * fields[1][j] for s, (i, j) in zip(sums, GRAM)
-        )
-        return pack_lanes(last, packed, x, 0, 1), sums
-
-    packed, sums = loop(basis, ((blank, blank), (blank,) * len(GRAM)))
-    second_a = send_sum(1, 0, to_row(sums))
-    YS[2, 0], YS[2, 1] = packed
+        return pack_lanes(last, packed, x, 0, 1)
+
+    second_a = send_sum(1, 0, to_row(loop(products, (blank,) * len(GRAM))))
+    YS[2, 0], YS[2, 1] = loop(keep_basis, (blank, blank))
     pack_rows(5, 1)
     sent = start_halo(2, 5, 1, 1)
     end_halo(sent, 5, 1, 1)

time: 46.2 us -> 46.2 us (level)
  no operation moved by 1% of the time
where the time goes in v6:
time: 46.2 us; the launch traced here: 46 us
  Pallas kernels  45.4 us (98%)
  between operations  0.64 us (1%)
    pallas_call x1, Pallas kernels, shards(): pl.pallas_call(main_kernel, out_shape=(pltpu.VMEM((6,) + inner, F32), plt...  44.3 us
    pallas_call x1, Pallas kernels, shards(): pl.pallas_call(combine_kernel, out_shape=(jax.ShapeDtypeStruct(block, F32...  1.06 us

profile of v6, /device:TPU:1, one launch (start us, length us, event | category | flops | bytes accessed | tf_op | source)
XLA Modules:
  0.0 46.0 jit_solution(17972995002953454124)
XLA Ops:
  0.6 44.3 %basis_and_sums.1 = (f32[6,24,2,8,128]{4,3,2,1,0:T(8,128)S(1)}, f32[19,8,128]{2,1,0:T(8,128)S(1)}) custom-call(f32[24,8,256]{2,1,0:T(8,128)} %b_hbm.1, f32[24,8,256]{2,1,0:T(8,128)} %k_hbm.1), custom_call_target="tpu_custom_call" | custom-call | tf_op jit(solution)/shard_map/basis_and_sums/pallas_call | solution.py:569
  45.0 1.1 %combine.1 = (f32[24,8,256]{2,1,0:T(8,128)}, f32[24,8,256]{2,1,0:T(8,128)}, f32[24,8,256]{2,1,0:T(8,128)}, f32[24,8,256]{2,1,0:T(8,128)}) custom-call(f32[6,24,2,8,128]{4,3,2,1,0:T(8,128)S(1)} %get-tuple-element.6.w_ref, f32[19,8,128]{2,1,0:T(8,128)S(1)} %get-tuple-element.7.coef_ref), custom_call_target="tpu_custom_call" | custom-call | tf_op jit(solution)/shard_map/combine/pallas_call | solution.py:603
